TPU v7x, 32 devices: a whole 2x2x4 slice. The times are simulated.
32 devices in a mesh: dp: 8 (over y, x, core), mp: 4 (over z).
Axes of the slice: x: 2, y: 2, z: 4, core: 2. Of those that a mesh axis runs over, the one named last changes fastest.
Arguments:
- block_input: bfloat16 [16384, 1536], P('dp', 'mp'), may hold values from -6 to 6
- row_order: int32 [16, 1024], P('dp'), may hold values from 0 to 1023, as said below
- conv_weight: bfloat16 [5, 1536, 1536], P(None, 'mp'), may hold values from -0.0625 to 0.0625
- batch_gain: float32 [1536], P('mp'), may hold values from 0.25 to 1.75
- batch_bias: float32 [1536], P('mp'), may hold values from -1.75 to 1.75
- first_gain: float32 [1536], replicated, may hold values from 0.25 to 1.75
- first_bias: float32 [1536], replicated, may hold values from -1.75 to 1.75
- w_query: bfloat16 [1536, 512], P(None, 'mp'), may hold values from -0.15625 to 0.15625
- w_key: bfloat16 [1536, 512], P(None, 'mp'), may hold values from -0.15625 to 0.15625
- w_value: bfloat16 [1536, 1536], P(None, 'mp'), may hold values from -0.15625 to 0.15625
- relative_weight: bfloat16 [192, 512], P(None, 'mp'), may hold values from -0.4375 to 0.4375
- content_bias: float32 [8, 64], P('mp'), may hold values from -0.875 to 0.875
- position_bias: float32 [8, 64], P('mp'), may hold values from -0.875 to 0.875
- w_out: bfloat16 [1536, 1536], P('mp'), may hold values from -1.25 to 1.25
- second_gain: float32 [1536], replicated, may hold values from 0.25 to 1.75
- second_bias: float32 [1536], replicated, may hold values from -1.75 to 1.75
- w_inner: bfloat16 [1536, 3072], P(None, 'mp'), may hold values from -0.15625 to 0.15625
- inner_bias: float32 [3072], P('mp'), may hold values from -1.75 to 1.75
- w_outer: bfloat16 [3072, 1536], P('mp'), may hold values from -0.109375 to 0.109375
- cotangent: bfloat16 [16384, 1536], P('dp'), may hold values from -7 to 7
Outputs:
- block_output: bfloat16 [16384, 1536], P(('dp', 'mp'))
- grad_input: float32 [16384, 1536], P('dp', 'mp')
- grad_conv: float32 [5, 1536, 1536], P(None, 'mp')
- grad_batch_gain: float32 [1536], P('mp')
- grad_batch_bias: float32 [1536], P('mp')
- grad_first_gain: float32 [1536], replicated
- grad_first_bias: float32 [1536], replicated
- grad_query: float32 [1536, 512], P(None, 'mp')
- grad_key: float32 [1536, 512], P(None, 'mp')
- grad_value: float32 [1536, 1536], P(None, 'mp')
- grad_relative: float32 [192, 512], P(None, 'mp')
- grad_content_bias: float32 [8, 64], P('mp')
- grad_position_bias: float32 [8, 64], P('mp')
- grad_projection: float32 [1536, 1536], P('mp')
- grad_second_gain: float32 [1536], replicated
- grad_second_bias: float32 [1536], replicated
- grad_inner: float32 [1536, 3072], P(None, 'mp')
- grad_inner_bias: float32 [3072], P('mp')
- grad_outer: float32 [3072, 1536], P('mp')
Inputs may be any that keep to these rules, and one draw needn't show every extreme that they name: `row_order`: each row holds every number of 0 to 1023 once: the positions cyclically shifted, and reversed in some rows.
All inputs are finite; a program needn't handle non-finite values.
Results may differ from a plain program's by a relative error of at most 0.01.
Values may be sent and summed in bfloat16 or wider, within the bound.
A program may use at most 256 MiB of HBM per device.

v0:
```python
import math

import jax
import jax.numpy as jnp
from jax import lax
from jax.sharding import PartitionSpec as P

EPSILON = 1e-05


def gelu(value):
    return value * jax.nn.sigmoid(1.702 * value)


def gelu_slope(value):
    sig = jax.nn.sigmoid(1.702 * value)
    return sig + 1.702 * value * sig * (1.0 - sig)


def norm_rows(rows, gain, bias):
    centre = rows - jnp.mean(rows, axis=-1, keepdims=True)
    spread = jnp.mean(centre * centre, axis=-1, keepdims=True)
    inverse = lax.rsqrt(spread + EPSILON)
    unit = centre * inverse
    return (unit * gain + bias, unit, inverse)


def norm_back(grad, unit, inverse, gain):
    scaled = grad * gain
    return inverse * (
        scaled
        - jnp.mean(scaled, axis=-1, keepdims=True)
        - unit * jnp.mean(scaled * unit, axis=-1, keepdims=True)
    )


def relative_basis(length, features):
    distance = jnp.arange(2 * length - 1, dtype=jnp.float32) - (length - 1)
    half = features // 2
    ratio = jnp.arange(half, dtype=jnp.float32) / (half - 1)
    life = jnp.power(jnp.float32(length), ratio)
    decay = jnp.exp(-math.log(2.0) * jnp.abs(distance)[:, None] / life[None, :])
    return jnp.concatenate([decay, jnp.sign(distance)[:, None] * decay], axis=1)


def rel_shift(window, length):
    heads, rows, width = window.shape
    padded_input = jnp.pad(window, ((0, 0), (0, 0), (0, 1)))
    flat = padded_input.reshape(heads, rows * (width + 1))
    taken = flat[:, rows - 1 : rows - 1 + rows * width]
    return taken.reshape(heads, rows, width)[:, :, :length]


def rel_unshift(grad, length):
    heads, rows, _ = grad.shape
    width = length + rows - 1
    padded_input = jnp.pad(grad, ((0, 0), (0, 0), (0, width - length)))
    flat = jnp.pad(padded_input.reshape(heads, rows * width), ((0, 0), (rows - 1, 1)))
    return flat.reshape(heads, rows, width + 1)[:, :, :width]


def place_share(values, groups, member):
    whole = jnp.zeros((values.shape[0] * groups,) + values.shape[1:], jnp.float32)
    return lax.dynamic_update_slice_in_dim(whole, values, member * values.shape[0], 0)


def take_share(values, count, member):
    return lax.dynamic_slice_in_dim(values, member * count, count, 0)


def sum_feed(g_inner, g_outer):
    return lax.psum((g_inner, g_outer), "dp")


def share_grads(g_conv, query_gradient, g_key, g_value, g_relative, g_out):
    shapes = (
        g_conv.shape,
        query_gradient.shape,
        g_key.shape,
        g_value.shape,
        g_relative.shape,
        g_out.shape,
    )
    parts = (
        lax.psum_scatter(g_conv.reshape(-1), "dp", scatter_dimension=0, tiled=True),
        lax.psum_scatter(query_gradient.reshape(-1), "dp", scatter_dimension=0, tiled=True),
        lax.psum_scatter(g_key.reshape(-1), "dp", scatter_dimension=0, tiled=True),
        lax.psum_scatter(g_value.reshape(-1), "dp", scatter_dimension=0, tiled=True),
        lax.psum_scatter(g_relative.reshape(-1), "dp", scatter_dimension=0, tiled=True),
        lax.psum_scatter(g_out.reshape(-1), "dp", scatter_dimension=0, tiled=True),
    )
    p_conv, p_query, p_key, p_value, p_relative, p_out = parts
    whole = (
        lax.all_gather(p_conv, "dp", axis=0, tiled=True),
        lax.all_gather(p_query, "dp", axis=0, tiled=True),
        lax.all_gather(p_key, "dp", axis=0, tiled=True),
        lax.all_gather(p_value, "dp", axis=0, tiled=True),
        lax.all_gather(p_relative, "dp", axis=0, tiled=True),
        lax.all_gather(p_out, "dp", axis=0, tiled=True),
    )
    return tuple((item.reshape(shape) for item, shape in zip(whole, shapes)))


def on_device(
    block_input,
    row_order,
    conv_weight,
    batch_gain,
    batch_bias,
    first_gain,
    first_bias,
    w_query,
    w_key,
    w_value,
    relative_weight,
    content_bias,
    position_bias,
    w_out,
    second_gain,
    second_bias,
    w_inner,
    inner_bias,
    w_outer,
    cotangent,
):
    f32 = jnp.float32
    bf16 = jnp.bfloat16
    seq_count, length = row_order.shape
    group_rows = seq_count * length
    own_cols = block_input.shape[1]
    width = conv_weight.shape[2]
    taps = conv_weight.shape[0]
    reach = taps // 2
    heads_here = content_bias.shape[0]
    key_size = content_bias.shape[1]
    value_size = w_value.shape[1] // heads_here
    groups = lax.axis_size("mp")
    member = lax.axis_index("mp")
    col_start = member * own_cols
    own_rows = group_rows // groups
    total_rows = group_rows * lax.axis_size("dp")
    scale = key_size ** (-0.5)
    block = min(512, length)
    per_seq = length // block
    blocks = seq_count * per_seq
    offsets = (jnp.arange(seq_count, dtype=jnp.int32) * length)[:, None]
    source = (row_order + offsets).reshape(group_rows)
    shifted = block_input[source].astype(f32)
    stats = lax.psum((jnp.sum(shifted, axis=0), jnp.sum(shifted * shifted, axis=0)), "dp")
    batch_mean = stats[0] / total_rows
    batch_var = stats[1] / total_rows - batch_mean * batch_mean
    batch_scale = lax.rsqrt(batch_var + EPSILON)
    centred = (shifted - batch_mean) * batch_scale
    pre_act = batch_gain * centred + batch_bias
    act = gelu(pre_act).astype(bf16)
    act_pad = jnp.pad(act.reshape(seq_count, length, own_cols), ((0, 0), (reach, reach), (0, 0)))
    conv_terms = jnp.zeros((seq_count, length, width), f32)
    for shift_amount in range(taps):
        conv_terms = conv_terms + jnp.einsum(
            "muk,kn->mun",
            act_pad[:, shift_amount : shift_amount + length],
            conv_weight[shift_amount],
            preferred_element_type=f32,
        )
    conv_terms = conv_terms.reshape(group_rows, width)
    own_part = lax.dynamic_slice_in_dim(conv_terms, col_start, own_cols, 1) + shifted
    conv_terms = lax.dynamic_update_slice_in_dim(conv_terms, own_part, col_start, 1)
    resid_one = lax.psum_scatter(conv_terms, "mp", scatter_dimension=0, tiled=True)
    normed_one, unit_one, inverse_one = norm_rows(resid_one, first_gain, first_bias)
    normed_one = normed_one.astype(bf16)
    rows_one = lax.all_gather(normed_one, "mp", axis=0, tiled=True)
    query = (
        jnp.dot(rows_one, w_query, preferred_element_type=f32).reshape(
            group_rows, heads_here, key_size
        )
        * scale
    )
    query_w = (query + content_bias).astype(bf16)
    query_r = (query + position_bias).astype(bf16)
    keys = (
        jnp.dot(rows_one, w_key, preferred_element_type=f32)
        .astype(bf16)
        .reshape(group_rows, heads_here, key_size)
    )
    values = (
        jnp.dot(rows_one, w_value, preferred_element_type=f32)
        .astype(bf16)
        .reshape(group_rows, heads_here, value_size)
    )
    basis = relative_basis(length, relative_weight.shape[0]).astype(bf16)
    rel_keys = (
        jnp.dot(basis, relative_weight, preferred_element_type=f32)
        .astype(bf16)
        .reshape(2 * length - 1, heads_here, key_size)
    )

    def block_logits(block_num):
        seq_num = block_num // per_seq
        first_row = block_num % per_seq * block
        row_base = seq_num * length + first_row
        block_w = lax.dynamic_slice_in_dim(query_w, row_base, block, 0)
        block_r = lax.dynamic_slice_in_dim(query_r, row_base, block, 0)
        seq_keys = lax.dynamic_slice_in_dim(keys, seq_num * length, length, 0)
        seq_values = lax.dynamic_slice_in_dim(values, seq_num * length, length, 0)
        window = lax.dynamic_slice_in_dim(
            rel_keys, length - first_row - block, length + block - 1, 0
        )
        content = jnp.einsum("rhd,khd->hrk", block_w, seq_keys, preferred_element_type=f32)
        position = rel_shift(
            jnp.einsum("rhd,whd->hrw", block_r, window, preferred_element_type=f32), length
        )
        return (
            content + position,
            block_w,
            block_r,
            seq_keys,
            seq_values,
            window,
            seq_num,
            first_row,
        )

    def attend(block_num):
        logits, block_w, block_r, seq_keys, seq_values, window, seq_num, first_row = block_logits(
            block_num
        )
        highest = jnp.max(logits, axis=-1, keepdims=True)
        weights = jnp.exp(logits - highest)
        totals = jnp.sum(weights, axis=-1, keepdims=True)
        prob = (weights / totals).astype(bf16)
        mixed = jnp.einsum("hrk,khd->rhd", prob, seq_values, preferred_element_type=f32)
        return (mixed.reshape(block, heads_here * value_size), (highest + jnp.log(totals))[..., 0])

    mixed_all, log_totals = lax.map(attend, jnp.arange(blocks, dtype=jnp.int32))
    attended = mixed_all.reshape(group_rows, heads_here * value_size).astype(bf16)
    resid_two = resid_one + lax.psum_scatter(
        jnp.dot(attended, w_out, preferred_element_type=f32), "mp", scatter_dimension=0, tiled=True
    )
    normed_two, unit_two, inverse_two = norm_rows(resid_two, second_gain, second_bias)
    normed_two = normed_two.astype(bf16)
    rows_two = lax.all_gather(normed_two, "mp", axis=0, tiled=True)
    inner = jnp.dot(rows_two, w_inner, preferred_element_type=f32) + inner_bias
    hidden = gelu(inner).astype(bf16)
    block_output = (
        resid_two
        + lax.psum_scatter(
            jnp.dot(hidden, w_outer, preferred_element_type=f32),
            "mp",
            scatter_dimension=0,
            tiled=True,
        )
    ).astype(bf16)
    g_outer = jnp.einsum("ri,rd->id", hidden, cotangent, preferred_element_type=f32)
    d_hidden = jnp.einsum("rd,id->ri", cotangent, w_outer, preferred_element_type=f32)
    d_inner = (d_hidden * gelu_slope(inner)).astype(bf16)
    g_inner_bias = jnp.sum(d_inner.astype(f32), axis=0)
    g_inner = jnp.einsum("rd,ri->di", rows_two, d_inner, preferred_element_type=f32)
    d_norm_two = lax.psum_scatter(
        jnp.einsum("ri,di->rd", d_inner, w_inner, preferred_element_type=f32),
        "mp",
        scatter_dimension=0,
        tiled=True,
    )
    g_second_gain = jnp.sum(d_norm_two * unit_two, axis=0)
    g_second_bias = jnp.sum(d_norm_two, axis=0)
    own_cotangent = lax.dynamic_slice_in_dim(cotangent, member * own_rows, own_rows, 0)
    d_resid_two = own_cotangent.astype(f32) + norm_back(
        d_norm_two, unit_two, inverse_two, second_gain
    )
    grad_att = lax.all_gather(d_resid_two.astype(bf16), "mp", axis=0, tiled=True)
    g_out = jnp.einsum("rv,rd->vd", attended, grad_att, preferred_element_type=f32)
    d_attended = jnp.einsum("rd,vd->rv", grad_att, w_out, preferred_element_type=f32).astype(bf16)
    d_attended = d_attended.reshape(blocks, block, heads_here, value_size)

    def attend_back(carry, inputs):
        d_keys, d_values, d_rel = carry
        block_num, d_mixed, log_total = inputs
        logits, block_w, block_r, seq_keys, seq_values, window, seq_num, first_row = block_logits(
            block_num
        )
        prob = jnp.exp(logits - log_total[..., None])
        d_prob = jnp.einsum("rhd,khd->hrk", d_mixed, seq_values, preferred_element_type=f32)
        d_logits = (prob * (d_prob - jnp.sum(d_prob * prob, axis=-1, keepdims=True))).astype(bf16)
        value_part = jnp.einsum(
            "hrk,rhd->khd", prob.astype(bf16), d_mixed, preferred_element_type=f32
        )
        key_part = jnp.einsum("hrk,rhd->khd", d_logits, block_w, preferred_element_type=f32)
        d_query_w = jnp.einsum("hrk,khd->rhd", d_logits, seq_keys, preferred_element_type=f32)
        d_window = rel_unshift(d_logits, length)
        d_query_r = jnp.einsum("hrw,whd->rhd", d_window, window, preferred_element_type=f32)
        window_part = jnp.einsum("hrw,rhd->whd", d_window, block_r, preferred_element_type=f32)
        seq_row = seq_num * length
        d_keys = lax.dynamic_update_slice_in_dim(
            d_keys, lax.dynamic_slice_in_dim(d_keys, seq_row, length, 0) + key_part, seq_row, 0
        )
        d_values = lax.dynamic_update_slice_in_dim(
            d_values,
            lax.dynamic_slice_in_dim(d_values, seq_row, length, 0) + value_part,
            seq_row,
            0,
        )
        rel_row = length - first_row - block
        d_rel = lax.dynamic_update_slice_in_dim(
            d_rel,
            lax.dynamic_slice_in_dim(d_rel, rel_row, length + block - 1, 0) + window_part,
            rel_row,
            0,
        )
        return ((d_keys, d_values, d_rel), (d_query_w, d_query_r))

    start_carry = (
        jnp.zeros((group_rows, heads_here, key_size), f32),
        jnp.zeros((group_rows, heads_here, value_size), f32),
        jnp.zeros((2 * length - 1, heads_here, key_size), f32),
    )
    (d_keys, d_values, d_rel), (d_query_w, d_query_r) = lax.scan(
        attend_back, start_carry, (jnp.arange(blocks, dtype=jnp.int32), d_attended, log_totals)
    )
    g_content = jnp.sum(d_query_w, axis=(0, 1))
    g_position = jnp.sum(d_query_r, axis=(0, 1))
    d_query = (
        ((d_query_w + d_query_r) * scale).astype(bf16).reshape(group_rows, heads_here * key_size)
    )
    d_keys = d_keys.astype(bf16).reshape(group_rows, heads_here * key_size)
    d_values = d_values.astype(bf16).reshape(group_rows, heads_here * value_size)
    query_gradient = jnp.einsum("rd,rq->dq", rows_one, d_query, preferred_element_type=f32)
    g_key = jnp.einsum("rd,rq->dq", rows_one, d_keys, preferred_element_type=f32)
    g_value = jnp.einsum("rd,rq->dq", rows_one, d_values, preferred_element_type=f32)
    g_relative = jnp.einsum(
        "wf,wq->fq",
        basis,
        d_rel.astype(bf16).reshape(2 * length - 1, heads_here * key_size),
        preferred_element_type=f32,
    )
    d_rows_one = jnp.einsum("rq,dq->rd", d_query, w_query, preferred_element_type=f32)
    d_rows_one = d_rows_one + jnp.einsum("rq,dq->rd", d_keys, w_key, preferred_element_type=f32)
    d_rows_one = d_rows_one + jnp.einsum("rq,dq->rd", d_values, w_value, preferred_element_type=f32)
    d_norm_one = lax.psum_scatter(d_rows_one, "mp", scatter_dimension=0, tiled=True)
    g_first_gain = jnp.sum(d_norm_one * unit_one, axis=0)
    g_first_bias = jnp.sum(d_norm_one, axis=0)
    d_resid_one = d_resid_two + norm_back(d_norm_one, unit_one, inverse_one, first_gain)
    grad_conv = lax.all_gather(d_resid_one.astype(bf16), "mp", axis=0, tiled=True)
    grad_seq = grad_conv.reshape(seq_count, length, width)
    grad_pad = jnp.pad(grad_seq, ((0, 0), (reach, reach), (0, 0)))
    conv_grads = []
    d_act = jnp.zeros((seq_count, length, own_cols), f32)
    for shift_amount in range(taps):
        conv_grads.append(
            jnp.einsum(
                "yxv,yxp->vp",
                act_pad[:, shift_amount : shift_amount + length],
                grad_seq,
                preferred_element_type=f32,
            )
        )
        d_act = d_act + jnp.einsum(
            "kyf,if->kyi",
            grad_pad[:, 2 * reach - shift_amount : 2 * reach - shift_amount + length],
            conv_weight[shift_amount],
            preferred_element_type=f32,
        )
    g_conv = jnp.stack(conv_grads).reshape(taps * own_cols, width)
    d_pre = d_act.reshape(group_rows, own_cols) * gelu_slope(pre_act)
    local_bias = jnp.sum(d_pre, axis=0)
    local_gain = jnp.sum(d_pre * centred, axis=0)
    summed = lax.psum(
        (
            place_share(local_gain, groups, member),
            place_share(local_bias, groups, member),
            g_first_gain,
            g_first_bias,
            g_second_gain,
            g_second_bias,
            place_share(g_content, groups, member),
            place_share(g_position, groups, member),
            place_share(g_inner_bias, groups, member),
        ),
        ("dp", "mp"),
    )
    g_batch_gain = take_share(summed[0], own_cols, member)
    g_batch_bias = take_share(summed[1], own_cols, member)
    d_shifted = lax.dynamic_slice_in_dim(grad_conv, col_start, own_cols, 1).astype(f32)
    d_shifted = d_shifted + batch_gain * batch_scale * (
        d_pre - g_batch_bias / total_rows - centred * g_batch_gain / total_rows
    )
    grad_input = jnp.zeros((group_rows, own_cols), f32).at[source].set(d_shifted)
    g_inner, g_outer = sum_feed(g_inner, g_outer)
    shared = share_grads(g_conv, query_gradient, g_key, g_value, g_relative, g_out)
    return (
        block_output,
        grad_input,
        shared[0].reshape(taps, own_cols, width),
        g_batch_gain,
        g_batch_bias,
        summed[2],
        summed[3],
        shared[1],
        shared[2],
        shared[3],
        shared[4],
        take_share(summed[6], heads_here, member),
        take_share(summed[7], heads_here, member),
        shared[5],
        summed[4],
        summed[5],
        g_inner,
        take_share(summed[8], w_inner.shape[1], member),
        g_outer,
    )


def solution(mesh):
    return jax.shard_map(
        on_device,
        mesh=mesh,
        in_specs=(
            P("dp", "mp"),
            P("dp", None),
            P(None, "mp", None),
            P("mp"),
            P("mp"),
            P(),
            P(),
            P(None, "mp"),
            P(None, "mp"),
            P(None, "mp"),
            P(None, "mp"),
            P("mp", None),
            P("mp", None),
            P("mp", None),
            P(),
            P(),
            P(None, "mp"),
            P("mp"),
            P("mp", None),
            P("dp", None),
        ),
        out_specs=(
            P(("dp", "mp"), None),
            P("dp", "mp"),
            P(None, "mp", None),
            P("mp"),
            P("mp"),
            P(),
            P(),
            P(None, "mp"),
            P(None, "mp"),
            P(None, "mp"),
            P(None, "mp"),
            P("mp", None),
            P("mp", None),
            P("mp", None),
            P(),
            P(),
            P(None, "mp"),
            P("mp"),
            P("mp", None),
        ),
        check_vma=False,
    )
```

profile of v0, /device:TPU:9, one launch (start us, length us, event | category | flops | bytes accessed | tf_op | source)
XLA Modules:
  0.0 2873.5 jit_solution(16375618631254470325)
XLA Ops:
  8.8 10.5 gather_fusion
  21.2 11.8 all-reduce.13
  65.4 23.0 add_add_fusion.1
  92.5 16.2 all-gather.8.cloned.1.call-start
  108.7 196.9 %reduce-scatter.6.cloned.1.call-done = f32[512,1536]{1,0:T(8,128)} async-done(((f32[2048,1536]{1,0:T(8,128)}), f32[512,1536]{1,0:T(8,128)}) %reduce-scatter.6.cloned.1.call-update) | async-done | bytes 3145744 | tf_op jit(solution)/shard_map/reduce_scatter | solution.py:168
  315.8 110.4 %all-gather.8.cloned.1.call-done = bf16[2048,1536]{1,0:T(8,128)(2,1)} async-done(((bf16[512,1536]{1,0:T(8,128)(2,1)}), bf16[2048,1536]{1,0:T(8,128)(2,1)}) %all-gather.8.cloned.1.call-update) | async-done | bytes 6291472 | tf_op jit(solution)/shard_map/all_gather | solution.py:171
  438.6 202.4 %while.38 = (s32[]{:T(128)}, bf16[4,512,384]{2,1,0:T(8,128)(2,1)}, f32[4,2,512]{2,1,0:T(2,128)S(1)}, s32[4]{0:T(128)S(1)}, bf16[2048,2,192]{0,2,1:T(8,128)(2,1)}...) while((s32[]{:T(128)}, bf16[4,512,384]{2,1,0:T(8,128)(2,1)}, ...), condition=%wide.region_10.11_spmd, body=%wide.region_7.10_spmd.sunk | while | flops 745405440 | bytes 83370544 | solution.py:234
  447.1 10.3 copy.102
  457.4 10.2 slice.213
  467.6 13.0 reshape.497
  497.6 10.3 copy.102
  507.9 10.2 slice.213
  518.1 13.0 reshape.497
  548.1 10.3 copy.102
  558.4 10.2 slice.213
  568.6 13.0 reshape.497
  598.6 10.3 copy.102
  608.9 10.2 slice.213
  619.1 13.0 reshape.497
  650.8 213.1 %reduce-scatter.8.cloned.1.call-done = f32[512,1536]{1,0:T(8,128)} async-done(((f32[2048,1536]{1,0:T(8,128)}), f32[512,1536]{1,0:T(8,128)}) %reduce-scatter.8.cloned.1.call-update) | async-done | bytes 3145744 | tf_op jit(solution)/shard_map/reduce_scatter | solution.py:236
  870.6 113.6 %all-gather.10.cloned.1.call-done = bf16[2048,1536]{1,0:T(8,128)(2,1)} async-done(((bf16[512,1536]{1,0:T(8,128)(2,1)}), bf16[2048,1536]{1,0:T(8,128)(2,1)}) %all-gather.10.cloned.1.call-update) | async-done | bytes 6291472 | tf_op jit(solution)/shard_map/all_gather | solution.py:241
  992.1 13.0 convert_reduce_fusion
  1015.2 12.8 fusion.154
  1028.1 200.2 %reduce-scatter.12.cloned.1.call-done = f32[512,1536]{1,0:T(8,128)} async-done(((f32[2048,1536]{1,0:T(8,128)}), f32[512,1536]{1,0:T(8,128)}) %reduce-scatter.12.cloned.1.call-update) | async-done | bytes 3145744 | tf_op jit(solution)/shard_map/reduce_scatter | solution.py:258
  1233.0 210.4 %reduce-scatter.10.cloned.1.call-done = f32[512,1536]{1,0:T(8,128)} async-done(((f32[2048,1536]{1,0:T(8,128)}), f32[512,1536]{1,0:T(8,128)}) %reduce-scatter.10.cloned.1.call-update) | async-done | bytes 3145744 | tf_op jit(solution)/shard_map/reduce_scatter | solution.py:246
  1450.1 113.6 %all-gather.12.cloned.1.call-done = bf16[2048,1536]{1,0:T(8,128)(2,1)} async-done(((bf16[512,1536]{1,0:T(8,128)(2,1)}), bf16[2048,1536]{1,0:T(8,128)(2,1)}) %all-gather.12.cloned.1.call-update) | async-done | bytes 6291472 | tf_op jit(solution)/shard_map/all_gather | solution.py:270
  1581.3 373.2 %while.39 = (s32[]{:T(128)}, f32[2048,2,64]{0,2,1:T(8,128)}, f32[2048,2,192]{0,2,1:T(8,128)}, f32[2047,2,64]{0,2,1:T(8,128)}, f32[4,512,2,64]{1,3,2,0:T(8,128)},...) while((s32[]{:T(128)}, f32[2048,2,64]{0,2,1:T(8,128)}, ...), condition=%wide.region_20.21_spmd, body=%wide.region_18.20_spmd.sunk | while | flops 1820654464 | bytes 213627824 | solution.py:316
  1607.7 10.3 copy.104
  1618.0 10.2 slice.217
  1628.2 12.9 reshape.498
  1696.2 10.3 copy.104
  1706.5 10.2 slice.217
  1716.7 12.9 reshape.498
  1785.2 10.3 copy.104
  1805.7 12.9 reshape.498
  1873.7 10.3 copy.104
  1894.2 12.9 reshape.498
  1966.2 11.4 add_add_fusion
  1977.7 213.1 %reduce-scatter.14.cloned.1.call-done = f32[512,1536]{1,0:T(8,128)} async-done(((f32[2048,1536]{1,0:T(8,128)}), f32[512,1536]{1,0:T(8,128)}) %reduce-scatter.14.cloned.1.call-update) | async-done | bytes 3145744 | tf_op jit(solution)/shard_map/reduce_scatter | solution.py:338
  2210.2 11.4 fusion.153
  2251.8 62.1 %all-gather.14.cloned.1.call-done = bf16[2048,1536]{1,0:T(8,128)(2,1)} async-done(((bf16[512,1536]{1,0:T(8,128)(2,1)}), bf16[2048,1536]{1,0:T(8,128)(2,1)}) %all-gather.14.cloned.1.call-update) | async-done | bytes 6291472 | tf_op jit(solution)/shard_map/all_gather | solution.py:342
  2337.6 13.0 reshape_reshape.6
  2352.5 339.3 %all-reduce.17.cloned.1.call-done = (f32[2949120]{0:T(1024)}, f32[196608]{0:T(1024)}, f32[196608]{0:T(1024)}, f32[589824]{0:T(1024)}, f32[24576]{0:T(1024)}, /*i...) async-done(((f32[2949120]{0:T(1024)}, f32[196608]{0:T(1024)}, f32[196608]{0:T(1024)}, f32[589824]{0:T(1024)}, f32[24576]{0:T(1024)}, ...) | async-done | bytes 27623440
  2735.5 41.5 %all-reduce.12 = (f32[1536]{0:T(1024)S(1)}, f32[1536]{0:T(1024)S(1)}, f32[1536]{0:T(1024)}, f32[1536]{0:T(1024)}, f32[8,64]{1,0:T(8,128)S(1)}, /*index=5*/f32[8,...) all-reduce(f32[1536]{0:T(1024)S(1)} %dynamic_update_slice.86, ...), channel_id=1, replica_groups=mesh['dp'=8,'mp'=4] {'dp','mp'}, use_global_device_ids=true, to_apply=%region_27.28 | all-reduce | flops 13312 | bytes 106496 | tf_op jit(solution)/shard_map/psum | solution.py:366
  2783.6 11.4 scatter_custom_fusion
  2797.0 15.6 all_gather.35
  2813.5 13.9 all_gather.36
  2843.6 13.4 reshape_reshape.7
  (486 shorter events, 576.7 us)
Async XLA Ops:
  7.2 984.9 %copy-start = (bf16[768,1536]{1,0:T(8,128)(2,1)S(1)}, bf16[768,1536]{1,0:T(8,128)(2,1)}, u32[]{:S(2)}) copy-start(bf16[768,1536]{1,0:T(8,128)(2,1)} %param.42) | copy-start | bytes 7077892
  7.2 298.4 %reduce-scatter.6.cloned.1.call-start = ((), (), s32[]{:S(2)}) async-start(), calls=%async_computation.5 | async-start | bytes 15728640 | tf_op jit(solution)/shard_map/reduce_scatter | solution.py:168
  8.8 24.2 copy-start.48
  8.8 24.8 copy-start.56
  39.1 13.5 copy-start.4
  65.4 23.0 copy-start.12
  92.5 218.3 %copy-start.41 = (f32[1536]{0:T(1024)S(1)}, f32[1536]{0:T(1024)}, u32[]{:S(2)}) copy-start(f32[1536]{0:T(1024)} %param.29) | copy-start | bytes 18436
  92.5 218.3 %copy-start.58 = (f32[1536]{0:T(1024)S(1)}, f32[1536]{0:T(1024)}, u32[]{:S(2)}) copy-start(f32[1536]{0:T(1024)} %param.30) | copy-start | bytes 18436
  92.5 333.7 %all-gather.8.cloned.1.call-start = ((), (), s32[]{:S(2)}) async-start(), calls=%async_computation.6 | async-start | bytes 7864320 | tf_op jit(solution)/shard_map/all_gather | solution.py:171
  312.5 113.7 %copy-start.32 = (bf16[1536,128]{1,0:T(8,128)(2,1)S(1)}, bf16[1536,128]{1,0:T(8,128)(2,1)}, u32[]{:S(2)}) copy-start(bf16[1536,128]{1,0:T(8,128)(2,1)} %param.31) | copy-start | bytes 1179652
  312.6 551.3 %reduce-scatter.8.cloned.1.call-start = ((), (), s32[]{:S(2)}) async-start(), calls=%async_computation.7 | async-start | bytes 15728640 | tf_op jit(solution)/shard_map/reduce_scatter | solution.py:236
  315.8 115.6 %copy-start.63 = (f32[2,64]{1,0:T(2,128)S(1)}, f32[2,64]{1,0:T(2,128)}, u32[]{:S(2)}) copy-start(f32[2,64]{1,0:T(2,128)} %param.36) | copy-start | bytes 1540
  315.8 115.6 %copy-start.64 = (f32[2,64]{1,0:T(2,128)S(1)}, f32[2,64]{1,0:T(2,128)}, u32[]{:S(2)}) copy-start(f32[2,64]{1,0:T(2,128)} %param.35) | copy-start | bytes 1540
  650.8 333.5 %all-gather.10.cloned.1.call-start = ((), (), s32[]{:S(2)}) async-start(), calls=%async_computation.8 | async-start | bytes 7864320 | tf_op jit(solution)/shard_map/all_gather | solution.py:241
  870.6 121.5 %copy-start.67 = (f32[768]{0:T(1024)S(1)}, f32[768]{0:T(1024)}, u32[]{:S(2)}) copy-start(f32[768]{0:T(1024)} %param.41) | copy-start | bytes 9220
  870.6 357.7 %reduce-scatter.12.cloned.1.call-start = ((), (), s32[]{:S(2)}) async-start(), calls=%async_computation.10 | async-start | bytes 15728640 | tf_op jit(solution)/shard_map/reduce_scatter | solution.py:258
  992.1 13.1 copy-start.71
  992.1 14.8 copy-start.65
  1015.1 428.3 %reduce-scatter.10.cloned.1.call-start = ((), (), s32[]{:S(2)}) async-start(), calls=%async_computation.9 | async-start | bytes 15728640 | tf_op jit(solution)/shard_map/reduce_scatter | solution.py:246
  1028.0 535.7 %all-gather.12.cloned.1.call-start = ((), (), s32[]{:S(2)}) async-start(), calls=%async_computation.11 | async-start | bytes 7864320 | tf_op jit(solution)/shard_map/all_gather | solution.py:270
  1450.1 740.7 %reduce-scatter.14.cloned.1.call-start = ((), (), s32[]{:S(2)}) async-start(), calls=%async_computation.12 | async-start | bytes 15728640 | tf_op jit(solution)/shard_map/reduce_scatter | solution.py:338
  1599.1 42.0 %copy-start.14 = (bf16[2048,2,64]{0,2,1:T(8,128)(2,1)}, bf16[2048,2,64]{0,2,1:T(8,128)(2,1)S(1)}, u32[]{:S(2)}) copy-start(bf16[2048,2,64]{0,2,1:T(8,128)(2,1)S(1)} %get-tuple-element.897) | copy-start | bytes 1572868 | tf_op jit(solution)/shard_map/while
  1599.1 45.2 %copy-start.21 = (bf16[4,512,2,192]{1,3,2,0:T(8,128)(2,1)}, bf16[4,512,2,192]{1,3,2,0:T(8,128)(2,1)S(1)}, u32[]{:S(2)}) copy-start(bf16[4,512,2,192]{1,3,2,0:T(8,128)(2,1)S(1)} %get-tuple-element.901) | copy-start | bytes 4718596 | tf_op jit(solution)/shard_map/while
  1687.6 42.0 %copy-start.14 = (bf16[2048,2,64]{0,2,1:T(8,128)(2,1)}, bf16[2048,2,64]{0,2,1:T(8,128)(2,1)S(1)}, u32[]{:S(2)}) copy-start(bf16[2048,2,64]{0,2,1:T(8,128)(2,1)S(1)} %get-tuple-element.897) | copy-start | bytes 1572868 | tf_op jit(solution)/shard_map/while
  1687.6 45.3 %copy-start.21 = (bf16[4,512,2,192]{1,3,2,0:T(8,128)(2,1)}, bf16[4,512,2,192]{1,3,2,0:T(8,128)(2,1)S(1)}, u32[]{:S(2)}) copy-start(bf16[4,512,2,192]{1,3,2,0:T(8,128)(2,1)S(1)} %get-tuple-element.901) | copy-start | bytes 4718596 | tf_op jit(solution)/shard_map/while
  1776.6 42.0 %copy-start.14 = (bf16[2048,2,64]{0,2,1:T(8,128)(2,1)}, bf16[2048,2,64]{0,2,1:T(8,128)(2,1)S(1)}, u32[]{:S(2)}) copy-start(bf16[2048,2,64]{0,2,1:T(8,128)(2,1)S(1)} %get-tuple-element.897) | copy-start | bytes 1572868 | tf_op jit(solution)/shard_map/while
  1776.6 45.3 %copy-start.21 = (bf16[4,512,2,192]{1,3,2,0:T(8,128)(2,1)}, bf16[4,512,2,192]{1,3,2,0:T(8,128)(2,1)S(1)}, u32[]{:S(2)}) copy-start(bf16[4,512,2,192]{1,3,2,0:T(8,128)(2,1)S(1)} %get-tuple-element.901) | copy-start | bytes 4718596 | tf_op jit(solution)/shard_map/while
  1865.0 42.0 %copy-start.14 = (bf16[2048,2,64]{0,2,1:T(8,128)(2,1)}, bf16[2048,2,64]{0,2,1:T(8,128)(2,1)S(1)}, u32[]{:S(2)}) copy-start(bf16[2048,2,64]{0,2,1:T(8,128)(2,1)S(1)} %get-tuple-element.897) | copy-start | bytes 1572868 | tf_op jit(solution)/shard_map/while
  1865.0 45.3 %copy-start.21 = (bf16[4,512,2,192]{1,3,2,0:T(8,128)(2,1)}, bf16[4,512,2,192]{1,3,2,0:T(8,128)(2,1)S(1)}, u32[]{:S(2)}) copy-start(bf16[4,512,2,192]{1,3,2,0:T(8,128)(2,1)S(1)} %get-tuple-element.901) | copy-start | bytes 4718596 | tf_op jit(solution)/shard_map/while
  1977.7 213.1 %copy-start.42 = (f32[1536]{0:T(1024)S(1)}, f32[1536]{0:T(1024)}, u32[]{:S(2)}) copy-start(f32[1536]{0:T(1024)} %param.29) | copy-start | bytes 18436
  1977.7 213.1 %copy-start.44 = (f32[512]{0:T(512)S(1)}, f32[512]{0:T(512)}, u32[]{:S(2)}) copy-start(f32[512]{0:T(512)} %copy-done.43) | copy-start | bytes 6148
  1977.7 213.2 %copy-start.55 = (f32[512]{0:T(512)S(1)}, f32[512]{0:T(512)}, u32[]{:S(2)}) copy-start(f32[512]{0:T(512)} %copy-done.54) | copy-start | bytes 6148
  1977.7 336.2 %all-gather.14.cloned.1.call-start = ((), (), s32[]{:S(2)}) async-start(), calls=%async_computation.13 | async-start | bytes 7864320 | tf_op jit(solution)/shard_map/all_gather | solution.py:342
  2200.2 10.0 copy-start.68
  2200.2 491.7 %all-reduce.17.cloned.1.call-start = ((), (), s32[]{:S(2)}) async-start(), calls=%async_computation.17 | async-start | bytes 55246848
  2200.2 21.4 slice-start.2
  2210.2 11.4 slice-start.3
  2210.2 11.4 copy-start.27
  2246.1 67.8 %copy-start.5 = (bf16[2,1024,384]{2,1,0:T(8,128)(2,1)S(1)}, bf16[2,1024,384]{2,1,0:T(8,128)(2,1)}, u32[]{:S(2)}) copy-start(bf16[2,1024,384]{2,1,0:T(8,128)(2,1)} %copy-done.4) | copy-start | bytes 4718596
  2350.6 349.4 %copy-start.62 = (f32[768]{0:T(1024)S(1)}, f32[768]{0:T(1024)}, u32[]{:S(2)}) copy-start(f32[768]{0:T(1024)} %get-tuple-element.640) | copy-start | bytes 9220
  2350.6 486.3 %all-gather.18.cloned.1.call-start = ((), (), s32[]{:S(2)}) async-start(), calls=%async_computation.15 | async-start | bytes 2654208 | tf_op jit(solution)/shard_map/all_gather | solution.py:97
  2693.6 146.8 %all-gather.20.cloned.1.call-start = ((), (), s32[]{:S(2)}) async-start(), calls=%async_computation.16 | async-start | bytes 2654208 | tf_op jit(solution)/shard_map/all_gather | solution.py:99
  2695.3 148.2 %all-gather.16.cloned.1.call-start = ((), (), s32[]{:S(2)}) async-start(), calls=%async_computation.14 | async-start | bytes 13271040 | tf_op jit(solution)/shard_map/all_gather | solution.py:94
  2700.3 14.6 slice-start
  2700.4 14.6 slice-start.4
  2725.5 10.0 copy-start.45
  2725.5 10.0 copy-start.46
  2725.5 52.9 %copy-start.61 = (f32[384]{0:T(512)S(1)}, f32[384]{0:T(512)}, u32[]{:S(2)}) copy-start(f32[384]{0:T(512)} %get-tuple-element.634) | copy-start | bytes 4612
  (81 other events, 272.0 us)
Sparse Core Ops, SparseCore 0:
  92.6 212.9 reduce-scatter.5
  312.7 113.4 all-gather.7
  650.9 212.9 reduce-scatter.7
  870.7 113.5 all-gather.9
  1015.3 212.9 reduce-scatter.11
  1230.5 212.8 reduce-scatter.9
  1450.2 113.4 all-gather.11
  1977.8 212.9 reduce-scatter.13
  2200.3 113.5 all-gather.13
  2350.8 341.0 all-reduce.16
  2694.3 29.1 all-gather.17
  2725.8 29.1 all-gather.19
  2756.9 75.7 all-gather.15
where the time goes:
time: 2890 us; the launch traced here: 2870 us
  waiting for transfers between devices  1770 us (61%)
  local copies, waits for them, and re-layouts  530 us (18%)
  matrix products  342 us (12%)
  blocking collectives  91.7 us (3%)
  other arithmetic  62.7 us (2%)
  loops' own time  40.3 us (1%)
    unnamed x14, waiting for transfers between devices  340 us
    reduce_scatter x1, waiting for transfers between devices, on_device(): lax.psum_scatter(jnp.dot(attended, w_out, preferred_element_type=f32), 'm...  213 us
    reduce_scatter x1, waiting for transfers between devices, on_device(): lax.psum_scatter(d_rows_one, 'mp', scatter_dimension=0, tiled=True)  213 us
    reduce_scatter x1, waiting for transfers between devices, on_device(): lax.psum_scatter(jnp.dot(hidden, w_outer, preferred_element_type=f32), 'm...  210 us
    reduce_scatter x1, waiting for transfers between devices, on_device(): lax.psum_scatter(jnp.einsum('ri,di->rd', d_inner, w_inner, preferred_elem...  200 us
    reduce_scatter x1, waiting for transfers between devices, on_device(): lax.psum_scatter(conv_terms, 'mp', scatter_dimension=0, tiled=True)  197 us
    while x120, local copies, waits for them, and re-layouts  162 us
    all_gather x1, waiting for transfers between devices, on_device(): rows_two = lax.all_gather(normed_two, 'mp', axis=0, tiled=True)  114 us
  transfers between devices with their start and end apart: 13, of which 10 were waited for; matrix products, arithmetic and copies ran while one was open for 5% of the time, Pallas kernels for 0%

commit v1 on v0

v1 whole, which is shorter than its diff:
```python
import functools
import math

import jax
import jax.numpy as jnp
from jax import lax
from jax.experimental import pallas as pl
from jax.experimental.pallas import tpu as pltpu
from jax.sharding import PartitionSpec as P

EPSILON = 1e-05
f32 = jnp.float32
bf16 = jnp.bfloat16
AXES = ("dp", "mp")
MESH = pl.DeviceIdType.MESH
NT = (((1,), (1,)), ((), ()))
TN = (((0,), (0,)), ((), ()))
NN = (((1,), (0,)), ((), ()))


def dot(a, b, dims=NN):
    return lax.dot_general(a, b, dims, preferred_element_type=f32)


def gelu(value):
    return value * jax.nn.sigmoid(1.702 * value)


def gelu_slope(value):
    sig = jax.nn.sigmoid(1.702 * value)
    return sig + 1.702 * value * sig * (1.0 - sig)


def norm_rows(rows, gain, bias):
    centre = rows - jnp.mean(rows, axis=-1, keepdims=True)
    spread = jnp.mean(centre * centre, axis=-1, keepdims=True)
    inverse = lax.rsqrt(spread + EPSILON)
    unit = centre * inverse
    return (unit * gain + bias, unit, inverse)


def norm_back(grad, unit, inverse, gain):
    scaled = grad * gain
    return inverse * (
        scaled
        - jnp.mean(scaled, axis=-1, keepdims=True)
        - unit * jnp.mean(scaled * unit, axis=-1, keepdims=True)
    )


def relative_basis(length, features):
    distance = jnp.arange(2 * length, dtype=f32) - (length - 1)
    half = features // 2
    ratio = jnp.arange(half, dtype=f32) / (half - 1)
    life = jnp.power(jnp.float32(length), ratio)
    decay = jnp.exp(-math.log(2.0) * jnp.abs(distance)[:, None] / life[None, :])
    return jnp.concatenate([decay, jnp.sign(distance)[:, None] * decay], axis=1)


def attend_kernel(dk, dv, bq, qw_ref, qr_ref, kv_ref, rel_ref, out_ref, prob_ref):
    rows, length = qw_ref.shape[1], kv_ref.shape[1]
    width = length + bq
    pair = qw_ref.shape[2] // dk
    lane = lax.broadcasted_iota(jnp.int32, (bq, pair * dk), 1) // dk
    keys = kv_ref[0, :, : pair * dk]
    for b in range(rows // bq):
        at = slice(b * bq, (b + 1) * bq)
        lo = rows - (b + 1) * bq
        window = rel_ref[0, lo : lo + width, :]
        qw, qr = qw_ref[0, at, :], qr_ref[0, at, :]
        zero = jnp.zeros_like(qw)
        mixed = []
        for h in range(pair):
            content = dot(jnp.where(lane == h, qw, zero), keys, NT)
            place = dot(jnp.where(lane == h, qr, zero), window, NT)
            place = pltpu.roll(place, width - (bq - 1), 1, stride=1, stride_axis=0)
            logits = content + place[:, :length]
            weights = jnp.exp(logits - jnp.max(logits, axis=1, keepdims=True))
            prob = (weights * (1.0 / jnp.sum(weights, axis=1, keepdims=True))).astype(bf16)
            prob_ref[0, h, at, :] = prob
            values = kv_ref[0, :, pair * dk + h * dv : pair * dk + (h + 1) * dv]
            mixed.append(dot(prob, values).astype(bf16))
        out_ref[0, at, :] = jnp.concatenate(mixed, axis=1)


def block_spec(*shape):
    return pl.BlockSpec((1,) + shape, lambda g: (g,) + (0,) * len(shape))


def attend(qw, qr, kv, rel, dk, dv, bq):
    groups, rows, qcols = qw.shape
    length, kvcols = kv.shape[1:]
    pair = qcols // dk
    return pl.pallas_call(
        functools.partial(attend_kernel, dk, dv, bq),
        grid=(groups,),
        in_specs=[
            block_spec(rows, qcols),
            block_spec(rows, qcols),
            block_spec(length, kvcols),
            block_spec(rel.shape[1], qcols),
        ],
        out_specs=[block_spec(rows, pair * dv), block_spec(pair, rows, length)],
        out_shape=[
            jax.ShapeDtypeStruct((groups, rows, pair * dv), bf16),
            jax.ShapeDtypeStruct((groups, pair, rows, length), bf16),
        ],
        compiler_params=pltpu.CompilerParams(vmem_limit_bytes=50 << 20),
    )(qw, qr, kv, rel)


def attend_back_kernel(
    dk, dv, bq, scale, qw_ref, qr_ref, kv_ref, rel_ref, prob_ref, dmix_ref,
    dq_ref, sums_ref, dkv_ref, drel_ref, dkt, dvt, drt,
):
    rows, length = qw_ref.shape[1], kv_ref.shape[1]
    width = length + bq
    pair = qw_ref.shape[2] // dk
    qcols = pair * dk
    lane = lax.broadcasted_iota(jnp.int32, (bq, qcols), 1) // dk
    across = lax.broadcasted_iota(jnp.int32, (bq, bq), 0)
    across = across + lax.broadcasted_iota(jnp.int32, (bq, bq), 1)
    flip = jnp.where(across == bq - 1, 1.0, 0.0).astype(bf16)
    keys = kv_ref[0, :, :qcols]
    sums_w = jnp.zeros((1, qcols), f32)
    sums_r = jnp.zeros((1, qcols), f32)
    drt[...] = jnp.zeros_like(drt)
    for b in range(rows // bq):
        at = slice(b * bq, (b + 1) * bq)
        lo = rows - (b + 1) * bq
        window = rel_ref[0, lo : lo + width, :]
        qw, qr = qw_ref[0, at, :], qr_ref[0, at, :]
        zero = jnp.zeros_like(qw)
        qr_flip = dot(flip, qr).astype(bf16)
        dqw = jnp.zeros((bq, qcols), f32)
        dqr = jnp.zeros((bq, qcols), f32)
        for h in range(pair):
            prob = prob_ref[0, h, at, :]
            values = kv_ref[0, :, qcols + h * dv : qcols + (h + 1) * dv]
            dmix = dmix_ref[0, at, h * dv : (h + 1) * dv]
            prob32 = prob.astype(f32)
            part = dot(dmix, values, NT) * prob32
            d_logits = part - prob32 * jnp.sum(part, axis=1, keepdims=True)
            d_logits = d_logits.astype(bf16)
            turned = jnp.concatenate(
                [dot(flip, d_logits), jnp.zeros((bq, width - length), f32)], axis=1
            )
            d_window = pltpu.roll(turned, 0, 1, stride=1, stride_axis=0).astype(bf16)
            dqw = dqw + jnp.where(lane == h, dot(d_logits, keys), 0.0)
            dqr = dqr + jnp.where(lane == h, dot(d_window, window), 0.0)
            key_part = dot(jnp.where(lane == h, qw, zero), d_logits, TN)
            value_part = dot(dmix, prob, TN)
            if b == 0 and h == 0:
                dkt[...] = key_part
            else:
                dkt[...] += key_part
            if b == 0:
                dvt[h] = value_part
            else:
                dvt[h] += value_part
            drt[:, lo : lo + width] += dot(jnp.where(lane == h, qr_flip, zero), d_window, TN)
        high = dqr.astype(bf16)
        dqr = dot(flip, high) + dot(flip, (dqr - high.astype(f32)).astype(bf16))
        sums_w += jnp.sum(dqw, axis=0, keepdims=True)
        sums_r += jnp.sum(dqr, axis=0, keepdims=True)
        dq_ref[0, at, :] = ((dqw + dqr) * scale).astype(bf16)
    sums_ref[0] = jnp.concatenate([sums_w, sums_r, jnp.zeros((6, qcols), f32)], axis=0)
    dkv_ref[0, :, :qcols] = dkt[...].T.astype(bf16)
    for h in range(pair):
        dkv_ref[0, :, qcols + h * dv : qcols + (h + 1) * dv] = dvt[h].T.astype(bf16)
    drel_ref[0] = drt[...].T.astype(bf16)


def attend_back(qw, qr, kv, rel, prob, dmix, dk, dv, bq, scale):
    groups, rows, qcols = qw.shape
    length, kvcols = kv.shape[1:]
    pair = qcols // dk
    rels = rel.shape[1]
    return pl.pallas_call(
        functools.partial(attend_back_kernel, dk, dv, bq, scale),
        grid=(groups,),
        in_specs=[
            block_spec(rows, qcols),
            block_spec(rows, qcols),
            block_spec(length, kvcols),
            block_spec(rels, qcols),
            block_spec(pair, rows, length),
            block_spec(rows, pair * dv),
        ],
        out_specs=[
            block_spec(rows, qcols),
            block_spec(8, qcols),
            block_spec(length, kvcols),
            block_spec(rels, qcols),
        ],
        out_shape=[
            jax.ShapeDtypeStruct((groups, rows, qcols), bf16),
            jax.ShapeDtypeStruct((groups, 8, qcols), f32),
            jax.ShapeDtypeStruct((groups, length, kvcols), bf16),
            jax.ShapeDtypeStruct((groups, rels, qcols), bf16),
        ],
        scratch_shapes=[
            pltpu.VMEM((qcols, length), f32),
            pltpu.VMEM((pair, dv, length), f32),
            pltpu.VMEM((qcols, rels), f32),
        ],
        compiler_params=pltpu.CompilerParams(vmem_limit_bytes=50 << 20),
    )(qw, qr, kv, rel, prob, dmix)


def line_of():
    core, level = lax.axis_index("dp") % 2, lax.axis_index("mp")
    depth = lax.axis_size("mp")
    rank = jnp.where(core == 0, level, depth - 1 - level)
    step = jnp.where(core == 0, 1, -1)
    place = lax.axis_index("dp")
    up, down, sibling = (place, level + step), (place, level - step), (place + 1 - 2 * core, level)
    return core, level, rank, up, down, sibling


def remote(src, dst, send_sem, recv_sem, device):
    return pltpu.make_async_remote_copy(
        src_ref=src,
        dst_ref=dst,
        send_sem=send_sem,
        recv_sem=recv_sem,
        device_id=device,
        device_id_type=MESH,
    )


def greet(rank, last, up, down, mates):
    barrier = pltpu.get_barrier_semaphore()

    @pl.when(rank < last)
    def _():
        pl.semaphore_signal(barrier, inc=1, device_id=up, device_id_type=MESH)

    @pl.when(rank > 0)
    def _():
        pl.semaphore_signal(barrier, inc=1, device_id=down, device_id_type=MESH)

    for mate in mates:
        pl.semaphore_signal(barrier, inc=1, device_id=mate, device_id_type=MESH)
    ends = (rank == 0) | (rank == last)
    pl.semaphore_wait(barrier, jnp.where(ends, 1 + len(mates), 2 + len(mates)))


def mate_of(place, level, bit):
    return place + (1 << bit) - (2 << bit) * (place // (1 << bit) % 2), level


class Both:
    def __init__(self, *copies):
        self.copies = copies

    def start(self):
        for copy in self.copies:
            copy.start()

    def wait_recv(self):
        for copy in self.copies:
            copy.wait_recv()

    def wait_send(self):
        for copy in self.copies:
            copy.wait_send()


def diagonal(size):
    row = lax.broadcasted_iota(jnp.int32, (1, size, size), 1)
    return jnp.where(row == lax.broadcasted_iota(jnp.int32, (1, size, size), 2), 1.0, 0.0)


def encode(rows, whole_ref, step_ref):
    step = jnp.max(jnp.abs(rows), axis=1, keepdims=True) * (1.0 / 32000.0)
    scaled = jnp.round(rows * (1.0 / jnp.maximum(step, 1e-30)))
    whole_ref[...] = scaled.astype(jnp.int32).astype(jnp.int16)
    step = step.reshape(rows.shape[0] // 128, 128, 1)
    step_ref[: step.shape[0], :] = jnp.sum(step * diagonal(128), axis=1)


def decode(whole_ref, step_ref):
    count = whole_ref.shape[0]
    step = step_ref[: count // 128, :].reshape(count // 128, 1, 128)
    step = jnp.sum(step * diagonal(128), axis=2, keepdims=True).reshape(count, 1)
    return whole_ref[...].astype(jnp.int32).astype(f32) * step


def front_kernel(
    chunk, taps, bits, total_rows,
    rows_ref, gain_ref, bias_ref, w_ref, share_ref, small_ref, cot_ref,
    resid_ref, act_ref, stats_ref, small_out, cot_out, weights_ref,
    acc, rx_far, rx_near, rx_back, tx_far, tx_near, stage, rx_half, tx_stats, rx_stats,
    rx_far_step, rx_near_step, rx_back_step, tx_far_step, tx_near_step,
    far_send, far_recv, near_send, near_recv, back_recv, swap_send, swap_recv,
    step_send, step_recv,
    stats_send, stats_recv, small_send, small_recv, cot_send, cot_recv, own_sem,
    up_send, down_send, level_recv, plane_send, plane_recv, cross_send, cross_recv,
    core_send, core_recv,
):
    core, level, rank, up, down, sibling = line_of()
    place = lax.axis_index("dp")
    levels = lax.axis_size("mp")
    own = place % 8
    seqs, length, own_cols = rows_ref.shape
    width = w_ref.shape[1]
    half = length // 2
    reach = taps // 2
    count = length // chunk
    per_half = count // 2
    tile = min(512, width)
    cut = width // 2
    mates = [mate_of(place, level, bit) for bit in range(bits)]

    barrier = pltpu.get_barrier_semaphore()
    for r in range(1, 4):
        other = (place, (level + r) % levels)
        pl.semaphore_signal(barrier, inc=1, device_id=other, device_id_type=MESH)
    for mate in mates:
        pl.semaphore_signal(barrier, inc=1, device_id=mate, device_id_type=MESH)

    values = rows_ref[...].astype(f32).reshape(seqs * length, own_cols)
    sums = jnp.sum(values, axis=0, keepdims=True)
    squares = jnp.sum(values * values, axis=0, keepdims=True)
    sums = jnp.concatenate([sums, squares, jnp.zeros((6, own_cols), f32)], axis=0)
    pl.semaphore_wait(barrier, 3 + bits)

    x_mate, y_mate = mates[1], mates[2]
    cross = [own + 2 - 4 * (own // 2 % 2), own + 4 - 8 * (own // 4)]
    corner = cross[0] + cross[1] - own
    left_half, right_half = slice(0, cut), slice(cut, width)

    def piece_at(q):
        base = jnp.where((level == 0) | (level == 3), q, jnp.where(q == 0, 1, jnp.where(q == 1, 0, q)))
        return jnp.where(level < 2, base, 3 - base)

    share_rows = share_ref.shape[0]

    def piece(z, block):
        return weights_ref.at[z, pl.ds(pl.multiple_of(block * share_rows, 16), share_rows)]

    def send(part, sems, device):
        return remote(part, part, sems[0], sems[1], device)

    def up_copy(z):
        return send(piece(z, own), (up_send.at[z], level_recv.at[z]), (place, level + 1))

    def down_copy(z):
        return send(piece(z, own), (down_send.at[z], level_recv.at[z]), (place, level - 1))

    def plane_copy(z, k):
        sems = (plane_send.at[z, k], plane_recv.at[z, k])
        return send(piece(z, own), sems, (x_mate, y_mate)[k])

    def cross_copy(z, k):
        part = piece(z, cross[1 - k]).at[:, (left_half, right_half)[k]]
        return send(part, (cross_send.at[z, k], cross_recv.at[z, k]), (x_mate, y_mate)[k])

    def core_copy(z, k):
        part = piece(z, (own, cross[0], cross[1], corner)[k])
        return send(part, (core_send.at[z, k], core_recv.at[z, k]), sibling)

    def weights_first(q):
        z = piece_at(q)

        @pl.when(z != level)
        def _():
            up_copy(z).wait_recv()

        @pl.when((z <= level) & (level < 3))
        def _():
            up_copy(z).start()

        @pl.when((z >= level) & (level > 0))
        def _():
            down_copy(z).start()

        plane_copy(z, 0).start()
        plane_copy(z, 1).start()
        core_copy(z, 0).start()

    def weights_second(q):
        z = piece_at(q)
        plane_copy(z, 0).wait_recv()
        plane_copy(z, 1).wait_recv()
        cross_copy(z, 0).start()
        cross_copy(z, 1).start()
        core_copy(z, 1).start()
        core_copy(z, 2).start()

    def weights_third(q):
        z = piece_at(q)
        cross_copy(z, 0).wait_recv()
        cross_copy(z, 1).wait_recv()
        core_copy(z, 3).start()

    def weights_fourth(q):
        z = piece_at(q)
        for k in range(4):
            core_copy(z, k).wait_recv()

    def weights_slot(t):
        for lag, part in enumerate((weights_first, weights_second, weights_third, weights_fourth)):
            if isinstance(t, int):
                if lag <= t < 4 + lag:
                    part(t - lag)
                continue

            @pl.when((t >= lag) & (t < 4 + lag))
            def _(lag=lag, part=part):
                part(t - lag)

    own_copy = pltpu.make_async_copy(share_ref, piece(level, own), own_sem)
    own_copy.start()

    def small_copy(r):
        other = (place, (level + r) % levels)
        sems = (small_send.at[r - 1], small_recv.at[level])
        return remote(small_ref, small_out.at[level], sems[0], sems[1], other)

    for r in range(1, 4):
        small_copy(r).start()
    small_out[level] = small_ref[...]
    cot_copy = remote(cot_ref.at[level % 2, 1 - core], cot_out, cot_send, cot_recv, sibling)
    cot_keep = pltpu.make_async_copy(cot_ref.at[level % 2, core], cot_out, cot_recv)

    @pl.when(rank < 2)
    def _():
        cot_copy.start()
        cot_keep.start()

    own_copy.wait()

    for bit in range(bits):
        tx_stats[bit] = sums
        copy = remote(
            tx_stats.at[bit], rx_stats.at[bit], stats_send.at[bit], stats_recv.at[bit], mates[bit]
        )
        copy.start()
        copy.wait()
        sums = sums + rx_stats[bit]
    weights_slot(0)
    mean = sums[0:1] / total_rows
    scale = lax.rsqrt(sums[1:2] / total_rows - mean * mean + EPSILON)
    stats_ref[...] = jnp.concatenate([mean, scale, jnp.zeros((6, own_cols), f32)], axis=0)
    row = lax.broadcasted_iota(jnp.int32, (length, own_cols), 0)
    for seq in range(seqs):
        centred = (rows_ref[seq].astype(f32) - mean) * scale
        act = gelu(gain_ref[...] * centred + bias_ref[...])
        for t in range(taps):
            moved = pltpu.roll(act, (reach - t) % length, 0) if t != reach else act
            inside = (row + (t - reach) >= 0) & (row + (t - reach) < length)
            act_ref[seq, :, t * own_cols : (t + 1) * own_cols] = jnp.where(
                inside, moved, 0.0
            ).astype(bf16)

    def line_copy(c, whole, step, sems, k, device):
        rows = pl.ds(pl.multiple_of(c * chunk, chunk), chunk)
        return Both(
            remote(whole[0].at[rows], whole[1].at[rows], sems[0].at[c], sems[1].at[c], device),
            remote(
                step[0].at[c], step[1].at[c], step_send.at[min(k, 1), c], step_recv.at[k, c], device
            ),
        )

    def far_copy(c):
        step = (tx_far_step, rx_far_step)
        return line_copy(c, (tx_far, rx_far), step, (far_send, far_recv), 0, down)

    def near_copy(c):
        step = (tx_near_step, rx_near_step)
        return line_copy(c, (tx_near, rx_near), step, (near_send, near_recv), 1, down)

    def back_copy(c):
        step = (tx_near_step, rx_back_step)
        return line_copy(c, (tx_near, rx_back), step, (near_send, back_recv), 2, up)

    def swap_copy(h):
        rows = pl.ds(h * chunk, chunk)
        return remote(stage.at[rows], rx_half.at[rows], swap_send.at[h], swap_recv.at[h], sibling)

    def finish(c):
        rows = pl.ds(c % per_half * chunk, chunk)

        @pl.when(c // per_half == core)
        def _():
            resid_ref[rows, :] = acc[...]

        @pl.when(c // per_half != core)
        def _():
            stage[rows, :] = acc[...]
            swap_copy(c % per_half).start()

    def step(i, _):
        @pl.when((rank == 0) & (i >= count))
        def _():
            weights_slot(i - count + 1)

        @pl.when(((rank == 1) | (rank == 2)) & (i % 2 == 1))
        def _():
            weights_slot(i // 2 + 1)

        c = i % count
        near = jnp.where(rank == 0, i < count, i >= count)
        seq = jnp.where(near, 1, 0)
        rows = pl.ds(pl.multiple_of(c * chunk, chunk), chunk)
        for n in range(width // tile):
            cols = slice(n * tile, (n + 1) * tile)
            acc[:, cols] = dot(act_ref[seq, rows, :], w_ref[:, cols])
        here = pl.ds(pl.multiple_of(level * own_cols, 128), own_cols)
        acc[:, here] += rows_ref[seq, rows, :].astype(f32)

        @pl.when(jnp.logical_not(near))
        def _():
            @pl.when(rank < 3)
            def _():
                far_copy(c).wait_recv()
                acc[...] += decode(rx_far.at[rows], rx_far_step.at[c])

            @pl.when(rank > 0)
            def _():
                encode(acc[...], tx_far.at[rows], tx_far_step.at[c])

                @pl.when(c >= 2)
                def _():
                    far_copy(c - 2).wait_send()

                far_copy(c).start()

            @pl.when(rank == 0)
            def _():
                finish(c)

                @pl.when(c >= 1)
                def _():
                    back_copy(c - 1).wait_send()

                back_copy(c).start()

        @pl.when(near)
        def _():
            @pl.when((rank == 1) | (rank == 2))
            def _():
                near_copy(c).wait_recv()
                acc[...] += decode(rx_near.at[rows], rx_near_step.at[c])

            @pl.when(rank == 1)
            def _():
                back_copy(c).wait_recv()
                acc[...] += decode(rx_back.at[rows], rx_back_step.at[c])
                finish(c)

            @pl.when(rank != 1)
            def _():
                encode(acc[...], tx_near.at[rows], tx_near_step.at[c])

            @pl.when(rank >= 2)
            def _():
                @pl.when(c < 2)
                def _():
                    far_copy(count - 2 + c).wait_send()

                @pl.when(c >= 2)
                def _():
                    near_copy(c - 2).wait_send()

                near_copy(c).start()

        return 0

    lax.fori_loop(0, 2 * count, step, 0)
    @pl.when(rank == 3)
    def _():
        lax.fori_loop(1, count + 1, lambda t, _: (weights_slot(t), 0)[1], 0)

    for t in range(count + 1, 7):
        weights_slot(t)

    @pl.when(rank >= 2)
    def _():
        def take(h, _):
            rows = pl.ds(pl.multiple_of(h * chunk, chunk), chunk)
            swap_copy(h).wait_recv()
            resid_ref[rows, :] = rx_half[rows, :]
            return 0

        lax.fori_loop(0, per_half, take, 0)
        cot_copy.wait_recv()

    @pl.when(rank < 2)
    def _():
        lax.fori_loop(0, per_half, lambda h, _: (swap_copy(h).wait_send(), 0)[1], 0)
        cot_copy.wait_send()
        cot_keep.wait()

    @pl.when(rank == 1)
    def _():
        far_copy(count - 2).wait_send()
        far_copy(count - 1).wait_send()

    @pl.when(rank >= 2)
    def _():
        near_copy(count - 2).wait_send()
        near_copy(count - 1).wait_send()

    @pl.when(rank == 0)
    def _():
        back_copy(count - 1).wait_send()

    for r in range(1, 4):
        small_copy(r).wait_send()
        other = (level + r) % levels
        part = small_out.at[other]
        remote(part, part, small_send.at[r - 1], small_recv.at[other], sibling).wait_recv()

    def end(z, _):
        @pl.when((z <= level) & (level < 3))
        def _():
            up_copy(z).wait_send()

        @pl.when((z >= level) & (level > 0))
        def _():
            down_copy(z).wait_send()

        for k in range(2):
            plane_copy(z, k).wait_send()
            cross_copy(z, k).wait_send()
        for k in range(4):
            core_copy(z, k).wait_send()
        return 0

    lax.fori_loop(0, levels, end, 0)


def whole_spec():
    return pl.BlockSpec(memory_space=pltpu.VMEM)


def any_spec():
    return pl.BlockSpec(memory_space=pl.ANY)


def front(rows, gain, bias, weight, share, small, cot, taps, bits, total_rows, chunk):
    seqs, length, own_cols = rows.shape
    depth, width = weight.shape
    levels = lax.axis_size("mp")
    half, count = length // 2, length // chunk
    dma = pltpu.SemaphoreType.DMA
    shape = jax.ShapeDtypeStruct
    return pl.pallas_call(
        functools.partial(front_kernel, chunk, taps, bits, total_rows),
        in_specs=[whole_spec()] * 6 + [any_spec()],
        out_specs=[whole_spec()] * 5 + [any_spec()],
        out_shape=[
            shape((half, width), f32),
            shape((seqs, length, depth), bf16),
            shape((8, own_cols), f32),
            shape((levels,) + small.shape, f32),
            shape((half, width), bf16),
            shape((levels, 8 * share.shape[0], width), bf16),
        ],
        scratch_shapes=[
            pltpu.VMEM((chunk, width), f32),
            pltpu.VMEM((length, width), jnp.int16),
            pltpu.VMEM((length, width), jnp.int16),
            pltpu.VMEM((length, width), jnp.int16),
            pltpu.VMEM((length, width), jnp.int16),
            pltpu.VMEM((length, width), jnp.int16),
            pltpu.VMEM((half, width), f32),
            pltpu.VMEM((half, width), f32),
            pltpu.VMEM((bits, 8, own_cols), f32),
            pltpu.VMEM((bits, 8, own_cols), f32),
            pltpu.VMEM((count, 8, 128), f32),
            pltpu.VMEM((count, 8, 128), f32),
            pltpu.VMEM((count, 8, 128), f32),
            pltpu.VMEM((count, 8, 128), f32),
            pltpu.VMEM((count, 8, 128), f32),
            dma((count,)),
            dma((count,)),
            dma((count,)),
            dma((count,)),
            dma((count,)),
            dma((count // 2,)),
            dma((count // 2,)),
            dma((2, count)),
            dma((3, count)),
            dma((bits,)),
            dma((bits,)),
            dma((3,)),
            dma((levels,)),
            dma(()),
            dma(()),
            dma(()),
            dma((levels,)),
            dma((levels,)),
            dma((levels,)),
            dma((levels, 2)),
            dma((levels, 2)),
            dma((levels, 2)),
            dma((levels, 2)),
            dma((levels, 4)),
            dma((levels, 4)),
        ],
        cost_estimate=pl.CostEstimate(
            flops=4 * length * depth * width, bytes_accessed=400 << 20, transcendentals=0
        ),
        compiler_params=pltpu.CompilerParams(
            collective_id=0, has_side_effects=True, vmem_limit_bytes=56 << 20
        ),
    )(rows, gain, bias, weight, share, small, cot)


def conv_back_kernel(
    chunk, taps, grad_ref, act_ref, w_ref, other_ref, dact_ref, dcol_ref, gw_ref, part_ref, rx_one,
    whole, gsum, acc, own_sum, loaded, rx_two, rx_three,
    half_send, half_recv, far_send, far_recv, near_send, near_recv, back_send, back_recv,
    keep_sem, out_sem, own_sem, load_sem, one_send, one_recv, two_send, two_recv, three_send, three_recv,
):
    core, level, rank, up, down, sibling = line_of()
    length, width = whole.shape[1:]
    half = length // 2
    own_cols = dcol_ref.shape[2]
    count = length // chunk
    reach = taps // 2
    tile = min(512, width)
    place = lax.axis_index("dp")
    x_mate, y_mate = mate_of(place, level, 1), mate_of(place, level, 2)
    b0, b1, b2 = place % 2, place // 2 % 2, place // 4 % 2
    levels = other_ref.shape[3]
    cut = width // 2
    left_half, right_half = slice(0, cut), slice(cut, width)
    greet(rank, 3, up, down, (sibling, x_mate, y_mate))

    def own_load(z):
        return pltpu.make_async_copy(other_ref.at[:, :, b0, z], own_sum.at[z], own_sem.at[z])

    def one_copy(z):
        part = other_ref.at[:, :, 1 - b0, z]
        return remote(part, rx_one.at[z], one_send.at[z], one_recv.at[z], sibling)

    def two_copy(z, k):
        if k == 0:
            part = own_sum.at[z, :, 1 - b1, :, left_half]
        else:
            part = own_sum.at[z, 1 - b2, :, :, right_half]
        sems = (two_send.at[z, k], two_recv.at[z, k])
        return remote(part, rx_two.at[z, k], sems[0], sems[1], (x_mate, y_mate)[k])

    def three_copy(z, k):
        if k == 0:
            part = own_sum.at[z, 1 - b2, b1, :, left_half]
        else:
            part = own_sum.at[z, b2, 1 - b1, :, right_half]
        sems = (three_send.at[z, k], three_recv.at[z, k])
        return remote(part, rx_three.at[z, k], sems[0], sems[1], (y_mate, x_mate)[k])

    def added(left, right):
        return (left.astype(f32) + right.astype(f32)).astype(bf16)

    def other_second(z):
        one_copy(z).wait_recv()
        load = pltpu.make_async_copy(rx_one.at[z], loaded, load_sem)
        load.start()
        own_load(z).wait()
        load.wait()
        own_sum[z] = added(own_sum[z], loaded[...])
        two_copy(z, 0).start()
        two_copy(z, 1).start()

    def other_third(z):
        two_copy(z, 0).wait_recv()
        two_copy(z, 1).wait_recv()
        for b in range(2):
            kept = own_sum[z, b, b1, :, left_half]
            own_sum[z, b, b1, :, left_half] = added(kept, rx_two[z, 0, b])
            kept = own_sum[z, b2, b, :, right_half]
            own_sum[z, b2, b, :, right_half] = added(kept, rx_two[z, 1, b])
        three_copy(z, 0).start()
        three_copy(z, 1).start()

    def other_fourth(z):
        three_copy(z, 0).wait_recv()
        three_copy(z, 1).wait_recv()
        part_ref[z, :, left_half] = added(own_sum[z, b2, b1, :, left_half], rx_three[z, 0])
        part_ref[z, :, right_half] = added(own_sum[z, b2, b1, :, right_half], rx_three[z, 1])

    def far_copy(c):
        rows = pl.ds(c * chunk, chunk)
        part = whole.at[0, rows]
        return remote(part, part, far_send.at[c], far_recv.at[c], up)

    def near_copy(c):
        rows = pl.ds(c * chunk, chunk)
        part = whole.at[1, rows]
        return remote(part, part, near_send.at[c], near_recv.at[c], up)

    def back_copy(c):
        rows = pl.ds(c * chunk, chunk)
        part = whole.at[1, rows]
        return remote(part, part, back_send.at[c], back_recv.at[c], down)

    slot = jnp.where((rank == 0) | (rank == 3), 0, 1)
    mine = whole.at[slot, pl.ds(core * half, half)]
    half_copy = remote(grad_ref, mine, half_send, half_recv, sibling)
    keep_copy = pltpu.make_async_copy(grad_ref, mine, keep_sem)

    @pl.when(rank >= 2)
    def _():
        half_copy.start()

    @pl.when(rank < 2)
    def _():
        keep_copy.start()

    for z in range(levels):
        one_copy(z).start()
        own_load(z).start()
    gsum[...] = jnp.zeros_like(gsum)
    acc[...] = jnp.zeros_like(acc)

    @pl.when(rank >= 2)
    def _():
        half_copy.wait_send()

    @pl.when(rank < 2)
    def _():
        keep_copy.wait()
        half_copy.wait_recv()

    def item(i):
        edge = (i == 0) | (i == 2 * count - 1)
        near = (i == 0) | ((i % 2 == 1) & (i != 2 * count - 1))
        c = jnp.where(edge, jnp.where(near, 0, count - 1), jnp.where(near, (i + 1) // 2, i // 2 - 1))
        return jnp.where(rank == 0, i >= count, near), jnp.where(rank == 0, i % count, c)

    def sent(i):
        near, c = item(i)

        @pl.when(near)
        def _():
            near_copy(c).wait_send()

        @pl.when(jnp.logical_not(near))
        def _():
            far_copy(c).wait_send()

    def step(i, _):
        @pl.when((i >= 1) & (i < 1 + levels))
        def _():
            other_second(i - 1)

        @pl.when((i >= 3) & (i < 3 + levels))
        def _():
            other_third(i - 3)

        @pl.when(i >= 5)
        def _():
            other_fourth(i - 5)

        near, c = item(i)
        seq = jnp.where(near, 1, 0)

        @pl.when(near)
        def _():
            @pl.when(rank >= 2)
            def _():
                near_copy(c).wait_recv()

            @pl.when(rank == 0)
            def _():
                back_copy(c).wait_recv()

        @pl.when(jnp.logical_not(near) & (rank > 0))
        def _():
            far_copy(c).wait_recv()

        @pl.when(((rank == 1) | (rank == 2)) & (i >= 2) | (rank == 0) & (i >= 2) & (i < count))
        def _():
            sent(i - 2)

        @pl.when(near & ((rank == 1) | (rank == 2)))
        def _():
            near_copy(c).start()

        @pl.when(near & (rank == 1))
        def _():
            @pl.when(c >= 2)
            def _():
                back_copy(c - 2).wait_send()

            back_copy(c).start()

        @pl.when(jnp.logical_not(near) & (rank < 3))
        def _():
            far_copy(c).start()

        rows = pl.ds(pl.multiple_of(c * chunk, chunk), chunk)
        grad = whole[seq, rows, :]
        own = pl.ds(pl.multiple_of(level * own_cols, 128), own_cols)
        dcol_ref[seq, rows, :] = whole[seq, rows, own]
        edge_rows = jnp.zeros((8, own_cols), f32)
        total = jnp.zeros((chunk + 16, own_cols), f32)
        for t in range(taps):
            term = dot(grad, w_ref[t * own_cols : (t + 1) * own_cols, :], NT)
            term = jnp.concatenate([edge_rows, term, edge_rows], axis=0)
            total = total + pltpu.roll(term, (t - reach) % (chunk + 16), 0)
        acc[seq, pl.ds(pl.multiple_of(c * chunk, 8), chunk + 16), :] += total
        for t in range(taps):
            left = act_ref[seq, rows, t * own_cols : (t + 1) * own_cols]
            for n in range(width // tile):
                cols = slice(n * tile, (n + 1) * tile)
                gsum[t * own_cols : (t + 1) * own_cols, cols] += dot(left, grad[:, cols], TN)
        return 0

    lax.fori_loop(0, 2 * count, step, 0)
    for z in range(2 * count - 5, levels):
        other_fourth(z)
    dact_out = pltpu.make_async_copy(acc.at[:, 8 : 8 + length], dact_ref, out_sem.at[0])
    dact_out.start()

    @pl.when(rank == 0)
    def _():
        sent(count - 2)
        sent(count - 1)

    @pl.when((rank == 1) | (rank == 2))
    def _():
        sent(2 * count - 2)
        sent(2 * count - 1)

    @pl.when(rank == 1)
    def _():
        back_copy(count - 2).wait_send()
        back_copy(count - 1).wait_send()

    for n in range(2):
        size = min(length, gsum.shape[0] - n * length)
        whole[n, :size] = gsum[n * length : n * length + size].astype(bf16)
        out = pltpu.make_async_copy(
            whole.at[n, :size], gw_ref.at[n * length : n * length + size], out_sem.at[1 + n]
        )
        out.start()
    for z in range(levels):
        one_copy(z).wait_send()
        for k in range(2):
            two_copy(z, k).wait_send()
            three_copy(z, k).wait_send()
    dact_out.wait()
    for n in range(2):
        size = min(length, gsum.shape[0] - n * length)
        pltpu.make_async_copy(
            whole.at[n, :size], gw_ref.at[n * length : n * length + size], out_sem.at[1 + n]
        ).wait()


def conv_back(grad, act_taps, weight, other, taps, chunk):
    seqs, length, depth = act_taps.shape
    width = weight.shape[1]
    own_cols = depth // taps
    count = length // chunk
    cell, levels, share, _ = other.shape
    dma = pltpu.SemaphoreType.DMA
    shape = jax.ShapeDtypeStruct
    return pl.pallas_call(
        functools.partial(conv_back_kernel, chunk, taps),
        in_specs=[any_spec(), whole_spec(), whole_spec(), any_spec()],
        out_specs=[any_spec(), whole_spec(), any_spec(), whole_spec(), any_spec()],
        out_shape=[
            shape((seqs, length, own_cols), f32),
            shape((seqs, length, own_cols), bf16),
            shape((depth, width), bf16),
            shape((levels, share, width), bf16),
            shape((levels, 2, 2, share, width), bf16),
        ],
        scratch_shapes=[
            pltpu.VMEM((seqs, length, width), bf16),
            pltpu.VMEM((depth, width), f32),
            pltpu.VMEM((seqs, length + 16, own_cols), f32),
            pltpu.VMEM((levels, 2, 2, share, width), bf16),
            pltpu.VMEM((2, 2, share, width), bf16),
            pltpu.VMEM((levels, 2, 2, share, width // 2), bf16),
            pltpu.VMEM((levels, 2, share, width // 2), bf16),
            dma(()),
            dma(()),
            dma((count,)),
            dma((count,)),
            dma((count,)),
            dma((count,)),
            dma((count,)),
            dma((count,)),
            dma(()),
            dma((3,)),
            dma((levels,)),
            dma(()),
            dma((levels,)),
            dma((levels,)),
            dma((levels, 2)),
            dma((levels, 2)),
            dma((levels, 2)),
            dma((levels, 2)),
        ],
        compiler_params=pltpu.CompilerParams(
            collective_id=1, has_side_effects=True, vmem_limit_bytes=58 << 20
        ),
    )(grad, act_taps, weight, other.reshape(2, 2, 2, levels, share, width))


def weight_grads_kernel(cell, count, *refs):
    out_ref, total = refs[-2], refs[-1]
    at = 0
    for i in range(count):
        left_ref, right_ref = refs[2 * i], refs[2 * i + 1]
        cols = left_ref.shape[2]
        tile = 256 if cols % 256 == 0 else 128
        for n in range(cols // tile):
            part = slice(n * tile, (n + 1) * tile)
            total[part, :] = dot(left_ref[0, :, part], right_ref[...], TN)
        rows = cols // cell
        for p in range(cell):
            out_ref[p, 0, at : at + rows, :] = total[p * rows : (p + 1) * rows, :].astype(bf16)
        at += rows
    if len(refs) > 2 * count + 2:
        extra_ref = refs[2 * count]
        out_ref[:, 0, at:, :] = extra_ref[:, 0]


def weight_grads(pairs, extra, cell):
    groups = pairs[0][0].shape[0]
    width = pairs[0][1].shape[1]
    rows = sum(left.shape[2] for left, _ in pairs) // cell
    specs, args = [], []
    for left, right in pairs:
        specs += [block_spec(*left.shape[1:]), pl.BlockSpec(right.shape, lambda g: (0, 0))]
        args += [left, right]
    if extra is not None:
        rows += extra.shape[2]
        specs.append(pl.BlockSpec((cell, 1) + extra.shape[2:], lambda g: (0, g, 0, 0)))
        args.append(extra)
    flops = sum(2 * left.size * width for left, _ in pairs)
    return pl.pallas_call(
        functools.partial(weight_grads_kernel, cell, len(pairs)),
        grid=(groups,),
        in_specs=specs,
        out_specs=pl.BlockSpec((cell, 1, rows, width), lambda g: (0, g, 0, 0)),
        out_shape=jax.ShapeDtypeStruct((cell, groups, rows, width), bf16),
        scratch_shapes=[pltpu.VMEM((max(left.shape[2] for left, _ in pairs), width), f32)],
        cost_estimate=pl.CostEstimate(flops=flops, bytes_accessed=30 << 20, transcendentals=0),
        compiler_params=pltpu.CompilerParams(vmem_limit_bytes=50 << 20),
    )(*args)


def last_sums_kernel(
    conv_ref, part_ref, conv_out, whole_out,
    total, rx_core, rx_two, tx_two, rx_three, tx_three, tx_line, rx_line,
    core_send, core_recv, two_send, two_recv, three_send, three_recv,
    back_send, back_recv, right_send, right_recv, left_send, left_recv, gather_send, gather_recv,
):
    place, level = lax.axis_index("dp"), lax.axis_index("mp")
    last = lax.axis_size("mp") - 1
    b0, b1, b2 = place % 2, place // 2 % 2, place // 4 % 2
    own = place % 8
    mates = [
        (place + 1 - 2 * b0, level),
        (place + 2 - 4 * b1, level),
        (place + 4 - 8 * b2, level),
    ]
    above, below = (place, level + 1), (place, level - 1)
    rows, width = conv_ref.shape
    r2, r4, r8 = rows // 2, rows // 4, rows // 8
    cut = width // 2
    halves = (slice(0, cut), slice(cut, width))
    bits = ((b1, b2), (b2, b1))
    across = ((mates[1], mates[2]), (mates[2], mates[1]))

    barrier = pltpu.get_barrier_semaphore()
    for mate in mates:
        pl.semaphore_signal(barrier, inc=1, device_id=mate, device_id_type=MESH)

    @pl.when(level < last)
    def _():
        pl.semaphore_signal(barrier, inc=1, device_id=above, device_id_type=MESH)

    @pl.when(level > 0)
    def _():
        pl.semaphore_signal(barrier, inc=1, device_id=below, device_id_type=MESH)

    pl.semaphore_wait(barrier, jnp.where((level == 0) | (level == last), 4, 5))

    def span(start, size):
        return pl.ds(pl.multiple_of(start, 16), size)

    mine = b0 * r2
    core_copy = remote(
        conv_ref.at[span((1 - b0) * r2, r2)], rx_core, core_send.at[0], core_recv.at[0], mates[0]
    )
    core_copy.start()

    def right(t, src):
        return remote(src, rx_line.at[t], right_send.at[t], right_recv.at[t], above)

    def left(t, src):
        slot = jnp.where(level - 1 == t, last + 1, t)
        return remote(src, rx_line.at[slot], left_send.at[t], left_recv.at[t], below)

    @pl.when(level == 0)
    def _():
        for t in range(last, 0, -1):
            right(t, part_ref.at[t]).start()

    @pl.when(level == last)
    def _():
        for t in range(last):
            left(t, part_ref.at[t]).start()

    def add_line(t):
        tx_line[t] = (part_ref[t].astype(f32) + rx_line[t].astype(f32)).astype(bf16)

    def pass_right(t, at):
        @pl.when(level == at)
        def _():
            right(t, part_ref.at[t]).wait_recv()
            add_line(t)
            right(t, tx_line.at[t]).start()

    def pass_left(t, at):
        @pl.when(level == at)
        def _():
            left(t, part_ref.at[t]).wait_recv()
            add_line(t)
            left(t, tx_line.at[t]).start()

    core_copy.wait_recv()
    total[...] = conv_ref[span(mine, r2), :].astype(f32) + rx_core[...].astype(f32)
    copies = []
    for h in range(2):
        first = bits[h][0]
        tx_two[h] = total[span((1 - first) * r4, r4), halves[h]].astype(bf16)
        copies.append(
            remote(tx_two.at[h], rx_two.at[h], two_send.at[h], two_recv.at[h], across[h][0])
        )
        copies[h].start()

    pass_right(3, 1)
    pass_left(0, 2)

    deeper = []
    for h in range(2):
        first, second = bits[h]
        copies[h].wait_recv()
        total[span(first * r4, r4), halves[h]] += rx_two[h].astype(f32)
        tx_three[h] = total[span(first * r4 + (1 - second) * r8, r8), halves[h]].astype(bf16)
        deeper.append(
            remote(
                tx_three.at[h], rx_three.at[h], three_send.at[h], three_recv.at[h], across[h][1]
            )
        )
        deeper[h].start()

    pass_right(3, 2)
    pass_left(0, 1)
    pass_right(2, 1)
    pass_left(1, 2)

    def back_copy(h, start, size, stage, mate):
        part = conv_out.at[span(start, size), halves[h]]
        return remote(part, part, back_send.at[stage, h], back_recv.at[stage, h], mate)

    stage_one, stage_two = [], []
    for h in range(2):
        first, second = bits[h]
        deeper[h].wait_recv()
        at = first * r4 + second * r8
        block = total[span(at, r8), halves[h]] + rx_three[h].astype(f32)
        conv_out[span(mine + at, r8), halves[h]] = block.astype(bf16)
        stage_one.append(back_copy(h, mine + at, r8, 0, across[h][1]))
        stage_one[h].start()
    for h in range(2):
        first = bits[h][0]
        stage_one[h].wait_recv()
        stage_two.append(back_copy(h, mine + first * r4, r4, 1, across[h][0]))
        stage_two[h].start()

    for t in range(last + 1):
        @pl.when(level == t)
        def _(t=t):
            block = part_ref[t].astype(f32)
            if t > 0:
                right(t, part_ref.at[t]).wait_recv()
                block = block + rx_line[t].astype(f32)
            if t < last:
                left(t, part_ref.at[t]).wait_recv()
                block = block + rx_line[last + 1].astype(f32)
            whole_out[own] = block.astype(bf16)

    def gather_copy(block, h, stage, mate):
        part = whole_out.at[block, :, halves[h]]
        k = 3 * h + stage
        return remote(part, part, gather_send.at[k], gather_recv.at[k], mate)

    one = own + 4 - 8 * b2, own + 2 - 4 * b1
    first_copies = [gather_copy(own, 0, 0, mates[2]), gather_copy(own, 1, 0, mates[1])]
    own_copies = [gather_copy(own, 0, 1, mates[1]), gather_copy(own, 1, 1, mates[2])]
    far_copies = [gather_copy(one[0], 0, 2, mates[1]), gather_copy(one[1], 1, 2, mates[2])]
    for h in range(2):
        first_copies[h].start()
        own_copies[h].start()

    for h in range(2):
        stage_two[h].wait_recv()
    region = conv_out.at[span(mine, r2)]
    core_back = remote(region, region, core_send.at[1], core_recv.at[1], mates[0])
    core_back.start()

    for h in range(2):
        first_copies[h].wait_recv()
        far_copies[h].start()

    def mate_copy(j, block):
        part = whole_out.at[block]
        return remote(part, part, gather_send.at[6 + j], gather_recv.at[6 + j], mates[0])

    blocks = [own, own + 2 - 4 * b1, own + 4 - 8 * b2, own + 6 - 4 * b1 - 8 * b2]
    mate_copies = [mate_copy(j, block) for j, block in enumerate(blocks)]
    mate_copies[0].start()
    for h in range(2):
        own_copies[h].wait_recv()
    mate_copies[1].start()
    mate_copies[2].start()
    for h in range(2):
        far_copies[h].wait_recv()
    mate_copies[3].start()

    core_copy.wait_send()
    core_back.wait()
    for j in range(4):
        mate_copies[j].wait()
    for h in range(2):
        copies[h].wait_send()
        deeper[h].wait_send()
        stage_one[h].wait_send()
        stage_two[h].wait_send()
        first_copies[h].wait_send()
        own_copies[h].wait_send()
        far_copies[h].wait_send()
    for t in range(last + 1):
        @pl.when(level < t)
        def _(t=t):
            right(t, part_ref.at[t]).wait_send()

        @pl.when(level > t)
        def _(t=t):
            left(t, part_ref.at[t]).wait_send()


def last_sums(conv, parts):
    rows, width = conv.shape
    levels, share, _ = parts.shape
    cut = width // 2
    dma = pltpu.SemaphoreType.DMA
    return pl.pallas_call(
        last_sums_kernel,
        in_specs=[whole_spec()] * 2,
        out_specs=[whole_spec()] * 2,
        out_shape=[
            jax.ShapeDtypeStruct((rows, width), bf16),
            jax.ShapeDtypeStruct((8, share, width), bf16),
        ],
        scratch_shapes=[
            pltpu.VMEM((rows // 2, width), f32),
            pltpu.VMEM((rows // 2, width), bf16),
            pltpu.VMEM((2, rows // 4, cut), bf16),
            pltpu.VMEM((2, rows // 4, cut), bf16),
            pltpu.VMEM((2, rows // 8, cut), bf16),
            pltpu.VMEM((2, rows // 8, cut), bf16),
            pltpu.VMEM((levels, share, width), bf16),
            pltpu.VMEM((levels + 1, share, width), bf16),
            dma((2,)),
            dma((2,)),
            dma((2,)),
            dma((2,)),
            dma((2,)),
            dma((2,)),
            dma((2, 2)),
            dma((2, 2)),
            dma((levels,)),
            dma((levels,)),
            dma((levels,)),
            dma((levels,)),
            dma((10,)),
            dma((10,)),
        ],
        compiler_params=pltpu.CompilerParams(
            collective_id=2, has_side_effects=True, vmem_limit_bytes=56 << 20
        ),
    )(conv, parts)


def on_device(
    block_input,
    row_order,
    conv_weight,
    batch_gain,
    batch_bias,
    first_gain,
    first_bias,
    w_query,
    w_key,
    w_value,
    relative_weight,
    content_bias,
    position_bias,
    w_out,
    second_gain,
    second_bias,
    w_inner,
    inner_bias,
    w_outer,
    cotangent,
):
    seq_count, length = row_order.shape
    group_rows = seq_count * length
    own_cols = block_input.shape[1]
    taps, _, width = conv_weight.shape
    reach = taps // 2
    pair, dk = content_bias.shape
    dv = w_value.shape[1] // pair
    qcols, vcols = pair * dk, pair * dv
    hidden_cols = w_inner.shape[1]
    features = relative_weight.shape[0]
    depth = lax.axis_size("mp")
    spread = lax.axis_size("dp")
    bits = spread.bit_length() - 1
    assert depth == 4 and seq_count == 2 and spread == 1 << bits and bits > 0
    place, level = lax.axis_index("dp"), lax.axis_index("mp")
    core = place % 2
    total_rows = group_rows * spread
    scale = dk ** (-0.5)
    half = length // 2


    def permute(value, route):
        pairs = []
        for d in range(spread):
            for z in range(depth):
                to = route(d, z)
                if to is not None:
                    pairs.append((d * depth + z, to[0] * depth + to[1]))
        return lax.ppermute(value, AXES, pairs)

    def swap_bit(value, bit):
        return permute(value, lambda d, z: (d ^ (1 << bit), z))

    def sum_dp(value):
        for bit in range(bits):
            value = value + swap_bit(value, bit)
        return value

    cell = min(8, spread)
    assert cell == 8
    cells = spread // cell
    inside = outside = None
    if cells > 1:
        inside = [[c * cell + i for i in range(cell)] for c in range(cells)]
        outside = [[c * cell + i for c in range(cells)] for i in range(cell)]

    def scatter_cell(value):
        value = lax.psum_scatter(value, "dp", scatter_dimension=0, axis_index_groups=inside)
        return value if cells == 1 else lax.psum(value, "dp", axis_index_groups=outside)

    order = jnp.where(core == 0, row_order, row_order[::-1])
    offsets = jnp.where(core == 0, jnp.array([0, length]), jnp.array([length, 0]))
    source = (order + offsets[:, None].astype(jnp.int32)).reshape(group_rows)
    rows = block_input[source].reshape(seq_count, length, own_cols)

    local = (w_inner.T, w_outer, w_out, jnp.concatenate([w_query.T, w_key.T, w_value.T], axis=0))
    local_rows = sum(value.shape[0] for value in local)
    share = lax.dynamic_slice_in_dim(
        jnp.concatenate(local, axis=0), place % cell * (local_rows // cell), local_rows // cell, 0
    )
    small = jnp.concatenate(
        [
            relative_weight.astype(f32),
            content_bias.reshape(1, qcols),
            position_bias.reshape(1, qcols),
            inner_bias.reshape(-1, qcols),
        ],
        axis=0,
    )
    conv_flat = conv_weight.reshape(taps * own_cols, width)
    resid_one, act_taps, stats, small, cot, weights = front(
        rows,
        batch_gain[None],
        batch_bias[None],
        conv_flat,
        share,
        small,
        cotangent.reshape(seq_count, 2, half, width),
        taps,
        bits,
        total_rows,
        min(256, half),
    )
    inner_weight = weights[:, :hidden_cols]
    outer_weight = weights[:, hidden_cols : 2 * hidden_cols]
    out_weight = weights[:, 2 * hidden_cols : 2 * hidden_cols + vcols]
    qkv_weight = weights[:, 2 * hidden_cols + vcols :]
    batch_mean, batch_scale = stats[0], stats[1]

    rel_weight = small[:, :features].astype(bf16)
    content_all = small[:, features][:, None, :]
    position_all = small[:, features + 1][:, None, :]
    inner_bias_all = small[:, features + 2 :].reshape(depth, 1, hidden_cols)
    basis = relative_basis(length, features)
    basis = jnp.where(jnp.arange(2 * length)[:, None] < 2 * length - 1, basis, 0.0).astype(bf16)
    basis = lax.dynamic_slice_in_dim(basis, half * (1 - core), length + half, 0)
    rel_keys = jnp.einsum(
        "wf,zfq->zwq", basis, rel_weight, preferred_element_type=f32
    ).astype(bf16)

    normed_one, unit_one, inverse_one = norm_rows(resid_one, first_gain, first_bias)
    normed_one = normed_one.astype(bf16)
    qkv = jnp.einsum("rd,znd->zrn", normed_one, qkv_weight, preferred_element_type=f32)
    query = qkv[:, :, :qcols] * scale
    query_w = (query + content_all).astype(bf16)
    query_r = (query + position_all).astype(bf16)
    kv_own = qkv[:, :, qcols:].astype(bf16)
    kv_other = swap_bit(kv_own, 0)
    kv = jnp.concatenate(
        [jnp.where(core == 0, kv_own, kv_other), jnp.where(core == 0, kv_other, kv_own)], axis=1
    )
    bq = min(256, half)
    attended, prob = attend(query_w, query_r, kv, rel_keys, dk, dv, bq)
    resid_two = resid_one + jnp.einsum(
        "zrn,znd->rd", attended, out_weight, preferred_element_type=f32
    )
    normed_two, unit_two, inverse_two = norm_rows(resid_two, second_gain, second_bias)
    normed_two = normed_two.astype(bf16)
    inner = (
        jnp.einsum("rd,znd->zrn", normed_two, inner_weight, preferred_element_type=f32)
        + inner_bias_all
    )
    hidden = gelu(inner).astype(bf16)
    block_output = (
        resid_two + jnp.einsum("zrn,znd->rd", hidden, outer_weight, preferred_element_type=f32)
    ).astype(bf16)
    block_output = permute(
        block_output, lambda d, z: (d - d % 2 + z // 2, 2 * (z % 2) + d % 2)
    )

    d_hidden = jnp.einsum("rd,znd->zrn", cot, outer_weight, preferred_element_type=f32)
    d_inner32 = d_hidden * gelu_slope(inner)
    d_inner = d_inner32.astype(bf16)
    g_inner_bias = jnp.sum(d_inner.astype(f32), axis=1)
    d_norm_two = jnp.einsum("zrn,znd->rd", d_inner, inner_weight, preferred_element_type=f32)
    feed_grads = weight_grads([(hidden, cot), (d_inner, normed_two)], None, cell)
    feed_parts = scatter_cell(feed_grads)
    g_second_gain = jnp.sum(d_norm_two * unit_two, axis=0)
    g_second_bias = jnp.sum(d_norm_two, axis=0)
    d_resid_two = cot.astype(f32) + norm_back(d_norm_two, unit_two, inverse_two, second_gain)

    d_two, _ = lax.optimization_barrier((d_resid_two.astype(bf16), feed_grads))
    d_attended = jnp.einsum("rd,znd->zrn", d_two, out_weight, preferred_element_type=f32)
    d_attended = d_attended.astype(bf16)
    d_query, query_sums, d_kv, d_rel = attend_back(
        query_w, query_r, kv, rel_keys, prob, d_attended, dk, dv, bq, scale
    )
    d_kv_give = lax.dynamic_slice_in_dim(d_kv, (1 - core) * half, half, 1)
    d_kv_keep = lax.dynamic_slice_in_dim(d_kv, core * half, half, 1)
    d_kv_own = (d_kv_keep.astype(f32) + swap_bit(d_kv_give, 0).astype(f32)).astype(bf16)
    d_qkv = jnp.concatenate([d_query, d_kv_own], axis=2)
    d_norm_one = jnp.einsum("zrn,znd->rd", d_qkv, qkv_weight, preferred_element_type=f32)
    g_first_gain = jnp.sum(d_norm_one * unit_one, axis=0)
    g_first_bias = jnp.sum(d_norm_one, axis=0)
    d_resid_one = (
        d_resid_two + norm_back(d_norm_one, unit_one, inverse_one, first_gain)
    ).astype(bf16)

    g_relative = jnp.einsum("wf,zwq->zfq", basis, d_rel, preferred_element_type=f32)
    of_level = jnp.concatenate(
        [
            g_relative.reshape(depth, -1),
            query_sums[:, 0],
            query_sums[:, 1],
            g_inner_bias,
        ],
        axis=1,
    )
    of_all = jnp.concatenate([g_first_gain, g_first_bias, g_second_gain, g_second_bias])
    of_all = jnp.broadcast_to(of_all[None], (depth, 4 * width))
    extra = jnp.concatenate([of_all, of_level], axis=1)
    used = extra.shape[1]
    extra_rows = -(-used // (cell * width))
    extra = jnp.pad(extra, ((0, 0), (0, extra_rows * cell * width - used)))
    extra = jnp.swapaxes(extra.reshape(depth, cell, extra_rows, width), 0, 1)
    extra = jnp.pad(extra, ((0, 0), (0, 0), (0, -extra_rows % 16), (0, 0))).astype(bf16)
    attend_grads = weight_grads([(attended, d_two), (d_qkv, normed_one)], extra, cell)

    d_act, d_cols, g_conv, attend_parts, _ = conv_back(
        d_resid_one, act_taps, conv_flat, attend_grads, taps, min(256, half)
    )
    d_act = d_act.reshape(group_rows, own_cols)
    centred = (rows.reshape(group_rows, own_cols).astype(f32) - batch_mean) * batch_scale
    pre_act = batch_gain * centred + batch_bias
    d_pre = d_act * gelu_slope(pre_act)
    batch_sums = sum_dp(jnp.stack([jnp.sum(d_pre * centred, axis=0), jnp.sum(d_pre, axis=0)]))
    g_batch_gain, g_batch_bias = batch_sums[0], batch_sums[1]
    d_shifted = d_cols.reshape(group_rows, own_cols).astype(f32)
    d_shifted = d_shifted + batch_gain * batch_scale * (
        d_pre - g_batch_bias / total_rows - centred * g_batch_gain / total_rows
    )
    grad_input = jnp.zeros((group_rows, own_cols), f32).at[source].set(d_shifted)

    if cells > 1:
        attend_parts = lax.psum(attend_parts, "dp", axis_index_groups=outside)
        g_conv = lax.psum(g_conv, "dp", axis_index_groups=outside)
    parts = jnp.concatenate([feed_parts, attend_parts], axis=1)
    g_conv, whole = last_sums(g_conv, parts)
    g_conv = g_conv.astype(f32).reshape(taps, own_cols, width)
    whole = whole.astype(f32)
    sums, at = [], 0
    for cols in (hidden_cols, hidden_cols, vcols, 2 * qcols + vcols):
        sums.append(whole[:, at : at + cols // cell].reshape(cols, width))
        at += cols // cell
    g_outer, g_inner, g_out, g_qkv = sums
    rest = whole[:, at : at + extra_rows].reshape(-1)[:used]

    def take(start, size):
        return rest[start : start + size]

    base = 4 * width
    rel_size = features * qcols

    return (
        block_output,
        grad_input,
        g_conv,
        g_batch_gain,
        g_batch_bias,
        take(0, width),
        take(width, width),
        g_qkv[:qcols].T,
        g_qkv[qcols : 2 * qcols].T,
        g_qkv[2 * qcols :].T,
        take(base, rel_size).reshape(features, qcols),
        take(base + rel_size, qcols).reshape(pair, dk),
        take(base + rel_size + qcols, qcols).reshape(pair, dk),
        g_out,
        take(2 * width, width),
        take(3 * width, width),
        g_inner.T,
        take(base + rel_size + 2 * qcols, hidden_cols),
        g_outer,
    )


def solution(mesh):
    return jax.shard_map(
        on_device,
        mesh=mesh,
        in_specs=(
            P("dp", "mp"),
            P("dp", None),
            P(None, "mp", None),
            P("mp"),
            P("mp"),
            P(),
            P(),
            P(None, "mp"),
            P(None, "mp"),
            P(None, "mp"),
            P(None, "mp"),
            P("mp", None),
            P("mp", None),
            P("mp", None),
            P(),
            P(),
            P(None, "mp"),
            P("mp"),
            P("mp", None),
            P("dp", None),
        ),
        out_specs=(
            P(("dp", "mp"), None),
            P("dp", "mp"),
            P(None, "mp", None),
            P("mp"),
            P("mp"),
            P(),
            P(),
            P(None, "mp"),
            P(None, "mp"),
            P(None, "mp"),
            P(None, "mp"),
            P("mp", None),
            P("mp", None),
            P("mp", None),
            P(),
            P(),
            P(None, "mp"),
            P("mp"),
            P("mp", None),
        ),
        check_vma=False,
    )
```

time: 2890 us -> 767 us (0.27)
  waiting for transfers between devices: 1770 us -> 3.34 us
  Pallas kernels: 0 us -> 523 us
  local copies, waits for them, and re-layouts: 530 us -> 80 us
  matrix products: 342 us -> 73.5 us
  blocking collectives: 91.7 us -> 0 us
  loops' own time: 40.3 us -> 0 us
    reduce_scatter x5 -> x1, waiting for transfers between devices: 1030 us -> 0.01 us  [scatter_cell(): lax.psum_scatter(value, 'dp', scatter_dimension=0, axis_index_groups=inside)]
    pallas_call x0 -> x7, Pallas kernels: none -> 523 us  [the longest x1 207 us: front(): pl.pallas_call(functools.partial(front_kernel, chunk, taps, bits, total_r...]
    all_gather x7 -> x0, waiting for transfers between devices: 400 us -> none  [the longest x1 114 us: on_device(): rows_two = lax.all_gather(normed_two, 'mp', axis=0, tiled=True)]
    unnamed x14 -> x1, waiting for transfers between devices: 340 us -> 0.02 us
    dot_general x79 -> x10, matrix products: 342 us -> 73.5 us  [the longest x1 11.2 us: on_device(): jnp.einsum('zrn,znd->rd', hidden, outer_weight, preferred_element_type=f32)]
    while x121 -> x0, local copies, waits for them, and re-layouts: 167 us -> none
    reshape x17 -> x6, local copies, waits for them, and re-layouts: 135 us -> 8.12 us  [the longest x1 6.04 us: on_device(): sums.append(whole[:, at:at + cols // cell].reshape(cols, width))]
    slice x8 -> x16, local copies, waits for them, and re-layouts: 81.6 us -> 18 us  [the longest x3 10.7 us: on_device(): sums.append(whole[:, at:at + cols // cell].reshape(cols, width))]
  transfers between devices with their start and end apart: 13 -> 7, of which waited for: 10 -> 3; matrix products, arithmetic and copies ran while one was open for 5% -> 10% of each run, Pallas kernels for 0% -> 21%
where the time goes in v1:
time: 767 us; the launch traced here: 758 us
  Pallas kernels  523 us (68%)
  local copies, waits for them, and re-layouts  80 us (10%)
  matrix products  73.5 us (10%)
  other arithmetic  57.6 us (8%)
  between operations  15.2 us (2%)
    pallas_call x1, Pallas kernels, front(): pl.pallas_call(functools.partial(front_kernel, chunk, taps, bits, total_r...  207 us
    pallas_call x1, Pallas kernels, last_sums(): pl.pallas_call(last_sums_kernel, in_specs=[whole_spec()] * 2, out_specs=[...  126 us
    pallas_call x1, Pallas kernels, conv_back(): pl.pallas_call(functools.partial(conv_back_kernel, chunk, taps), in_specs...  120 us
    unnamed x100, local copies, waits for them, and re-layouts  31.6 us
    pallas_call x1, Pallas kernels, attend_back(): pl.pallas_call(functools.partial(attend_back_kernel, dk, dv, bq, scale),...  25.8 us
    pallas_call x2, Pallas kernels, weight_grads(): pl.pallas_call(functools.partial(weight_grads_kernel, cell, len(pairs)),...  25.5 us
    pallas_call x1, Pallas kernels, attend(): pl.pallas_call(functools.partial(attend_kernel, dk, dv, bq), grid=(groups...  19 us
  transfers between devices with their start and end apart: 7, of which 3 were waited for; matrix products, arithmetic and copies ran while one was open for 10% of the time, Pallas kernels for 21%

profile of v1, /device:TPU:9, one launch (start us, length us, event | category | flops | bytes accessed | tf_op | source)
XLA Modules:
  0.0 758.0 jit_solution(9856675979495062183)
XLA Ops:
  11.4 2.8 rev.3
  15.0 1.4 convert_element_type.82
  18.8 1.6 copy.54
  20.4 4.3 copy.51
  24.7 3.2 bitcast_dynamic-update-slice_fusion
  27.9 9.1 %gather_fusion = bf16[2048,384]{1,0:T(8,128)(2,1)} fusion(bf16[2048,384]{1,0:T(8,128)(2,1)S(1)} %copy-done, s32[2048]{0:T(1024)S(1)} %broadcast_clamp_fusion), kind=kCustom, calls=%fused_computation | custom fusion | bytes 3153920 | tf_op jit(solution)/shard_map/gather | solution.py:1374
  37.0 3.3 constant_dynamic-update-slice_fusion.1
  44.0 2.2 constant_dynamic-slice_fusion.1.share_ref
  46.9 207.3 %shard_map.357 = (f32[512,1536]{1,0:T(8,128)}, bf16[2,1024,1920]{2,1,0:T(8,128)(2,1)}, f32[8,384]{1,0:T(8,128)}, f32[4,200,128]{2,1,0:T(8,128)}, bf16[512,1536]{...) custom-call(bf16[2,1024,384]{2,1,0:T(8,128)(2,1)} %bitcast.129, f32[1,384]{1,0:T(1,128)} %broadcast_in_dim.20.gain_ref, ...), custom_call_target="tpu_custom_call" | custom-call | flops 12079595520 | bytes 419430400 | tf_op jit(solution)/shard_map/pallas_call | solution.py:651
  254.2 2.3 reduce_sum.135
  258.1 7.3 fusion.46
  265.5 2.3 copy-done.19
  269.6 1.4 add_convert_fusion.4
  271.4 1.8 fusion.43.rel_ref
  273.2 3.2 broadcast_select_fusion.1
  276.4 2.3 pad_maximum_fusion.kv_ref
  278.7 19.0 %shard_map.358 = (bf16[4,512,384]{2,1,0:T(8,128)(2,1)S(1)}, bf16[4,2,512,1024]{3,2,1,0:T(8,128)(2,1)}) custom-call(bf16[4,512,128]{2,1,0:T(8,128)(2,1)S(1)} %get-tuple-element.77.qw_ref, bf16[4,512,128]{2,1,0:T(8,128)(2,1)S(1)} %get-tuple-element.76.qr_ref, bf16[4,1024,512]{2,1,0:T(8,128)(2,1)} %pad_maximum_fusion.kv_ref, bf16[4,1536,128]{2,1,0:T(8,128)(2,1)} %fusion.43.rel_ref), custom_call_target="tpu_custom_call" | custom-call | tf_op jit(solution)/shard_map/pallas_call | solution.py:94
  297.7 5.2 fusion.76
  304.4 10.0 %fusion.13 = (bf16[4,512,768]{2,1,0:T(8,128)(2,1)}, f32[4,768,512]{1,2,0:T(8,128)S(1)}) fusion(f32[4,768]{1,0:T(4,128)S(1)} %bitcast.145, bf16[512,1536]{1,0:T(8,128)(2,1)S(1)} %add_convert_fusion.2.refs_3_, bf16[4,2560,1536]{2,1,0:T(8,128)(2,1)} %get-tuple-element.39), kind=kOutput, calls=%fused_computation.18 | convolution fusion | flops 4842848256 | bytes 20459520 | tf_op jit(solution)/shard_map/rd,znd->zrn/dot_general | solution.py:1440
  314.4 10.2 %fusion.77 = (bf16[4,768]{1,0:T(4,128)(2,1)S(1)}, bf16[4,512,768]{2,1,0:T(8,128)(2,1)}) fusion(f32[4,768,512]{1,2,0:T(8,128)S(1)} %get-tuple-element.97, f32[4,768]{1,0:T(4,128)S(1)} %bitcast.146, bf16[512,1536]{1,0:T(8,128)(2,1)S(1)} %copy-done.2, bf16[4,2560,1536]{2,1,0:T(8,128)(2,1)} %get-tuple-element.39), kind=kOutput, calls=%fused_computation.135 | convolution fusion | flops 4850709504 | bytes 20465664 | tf_op jit(solution)/shard_map/rd,znd->zrn/dot_general | solution.py:1451
  324.6 14.2 %shard_map.359 = bf16[8,4,192,1536]{3,2,1,0:T(8,128)(2,1)} custom-call(bf16[4,512,768]{2,1,0:T(8,128)(2,1)} %get-tuple-element.96.refs_0_, bf16[512,1536]{1,0:T(8,128)(2,1)S(1)} %copy-done.2, bf16[4,512,768]{2,1,0:T(8,128)(2,1)} %get-tuple-element.101.refs_2_, bf16[512,1536]{1,0:T(8,128)(2,1)S(1)} %add_convert_fusion.2.refs_3_), custom_call_target="tpu_custom_call" | custom-call | flops 9663676416 | bytes 31457280 | tf_op jit(solution)/shard_map/pallas_call | solution.py:1041
  338.8 9.9 %multiply_reduce_fusion.1 = (bf16[1536]{0:T(1024)(128)(2,1)S(1)}, f32[512]{0:T(512)S(1)}, f32[512]{0:T(512)S(1)}, bf16[1536]{0:T(1024)(128)(2,1)S(1)}, f32[512,1536]{1,0:T(8,128)S(1)}) fusion(f32[512,1536]{1,0:T(8,128)} %copy-done.12, f32[512]{0:T(512)S(1)} %add_rsqrt_fusion, f32[512]{0:T(512)S(1)} %broadcast_multiply_fusion.5, f32[1536]{0:T(1024)S(1)} %copy-done.25, ...), kind=kOutput, calls=%fused_computation.43 | convolution fusion | flops 4838912000 | bytes 18894848 | tf_op jit(solution)/shard_map/zrn,znd->rd/dot_general | solution.py:1455
  348.8 2.6 fusion.69
  351.3 7.6 %fusion.57.dmix_ref = bf16[4,512,384]{2,1,0:T(8,128)(2,1)} fusion(bf16[512,1536]{1,0:T(8,128)(2,1)S(1)} %get-tuple-element.44.refs_1_, bf16[4,2560,1536]{2,1,0:T(8,128)(2,1)} %get-tuple-element.39), kind=kOutput, calls=%fused_computation.73 | convolution fusion | flops 2416705536 | bytes 7864320 | tf_op jit(solution)/shard_map/rd,znd->zrn/dot_general | solution.py:1463
  359.0 25.8 %shard_map.360 = (bf16[4,512,128]{2,1,0:T(8,128)(2,1)S(1)}, f32[4,8,128]{2,1,0:T(8,128)S(1)}, bf16[4,1024,512]{2,1,0:T(8,128)(2,1)}, bf16[4,1536,128]{2,1,0:T(8,128)(2,1)S(1)}) custom-call(bf16[4,512,128]{2,1,0:T(8,128)(2,1)S(1)} %get-tuple-element.77.qw_ref, bf16[4,512,128]{2,1,0:T(8,128)(2,1)S(1)} %get-tuple-element.76.qr_ref, ...), custom_call_target="tpu_custom_call" | custom-call | tf_op jit(solution)/shard_map/pallas_call | solution.py:179
  384.7 3.0 constant_dynamic-slice_fusion
  388.6 11.2 %fusion.40 = bf16[512,1536]{1,0:T(8,128)(2,1)} fusion(f32[512,1536]{1,0:T(8,128)} %copy-done.12, bf16[4,512,768]{2,1,0:T(8,128)(2,1)} %get-tuple-element.96.refs_0_, bf16[4,2560,1536]{2,1,0:T(8,128)(2,1)} %get-tuple-element.39), kind=kOutput, calls=%fused_computation.54 | convolution fusion | flops 4833411072 | bytes 17301504 | tf_op jit(solution)/shard_map/zrn,znd->rd/dot_general | solution.py:1445
  399.8 2.1 collective-permute-start.1
  402.5 2.5 add_convert_fusion
  405.2 9.7 %multiply_reduce_fusion.2 = (bf16[1536]{0:T(1024)(128)(2,1)S(1)}, f32[512]{0:T(512)S(1)}, f32[512]{0:T(512)S(1)}, bf16[1536]{0:T(1024)(128)(2,1)S(1)}, f32[512,1536]{1,0:T(8,128)}) fusion(f32[512,1536]{1,0:T(8,128)S(1)} %copy-done.9, f32[512]{0:T(512)S(1)} %copy-done.34, f32[512]{0:T(512)S(1)} %copy-done.31, f32[1536]{0:T(1024)S(1)} %copy-done.29, ...), kind=kOutput, calls=%fused_computation.44 | convolution fusion | flops 4038848512 | bytes 16797696 | tf_op jit(solution)/shard_map/zrn,znd->rd/dot_general | solution.py:1472
  417.1 1.8 pad_maximum_fusion.2.refs_2_
  420.1 4.2 add_convert_fusion.1.grad_ref
  424.3 11.3 %shard_map.361 = bf16[8,4,144,1536]{3,2,1,0:T(8,128)(2,1)} custom-call(bf16[4,512,384]{2,1,0:T(8,128)(2,1)S(1)} %copy-done.6, bf16[512,1536]{1,0:T(8,128)(2,1)S(1)} %copy-done.4, bf16[4,512,640]{2,1,0:T(8,128)(2,1)} %pad_maximum_fusion.2.refs_2_, bf16[512,1536]{1,0:T(8,128)(2,1)} %copy-done.21, bf16[8,4,16,1536]{3,2,1,0:T(8,128)(2,1)} %pad.11.refs_4_), custom_call_target="tpu_custom_call" | custom-call | flops 6442450944 | bytes 31457280 | tf_op jit(solution)/shard_map/pallas_call | solution.py:1041
  435.6 120.0 %shard_map.362 = (f32[2,1024,384]{2,1,0:T(8,128)}, bf16[2,1024,384]{2,1,0:T(8,128)(2,1)}, bf16[1920,1536]{1,0:T(8,128)(2,1)}, bf16[4,144,1536]{2,1,0:T(8,128)(2,1)}, bf16[4,2,2,144,1536]{4,3,2,1,0:T(8,128)(2,1)}) custom-call(bf16[512,1536]{1,0:T(8,128)(2,1)} %add_convert_fusion.1.grad_ref, bf16[2,1024,1920]{2,1,0:T(8,128)(2,1)} %get-tuple-element.47.act_ref, ...), custom_call_target="tpu_custom_call" | custom-call | tf_op jit(solution)/shard_map/pallas_call | solution.py:965
  555.7 4.0 multiply_reduce_fusion
  563.5 1.5 collective-permute-start.5
  566.6 2.4 fusion.39
  569.1 11.5 %scatter_custom_fusion = f32[2048,384]{1,0:T(8,128)} fusion(s32[2048]{0:T(1024)} %bitcast.143, f32[2048,384]{1,0:T(8,128)S(1)} %fusion.39, bf16[2048,384]{1,0:T(8,128)(2,1)} %bitcast.139, f32[]{:T(128)} %constant.76.clone.1), kind=kCustom, calls=%fused_computation.35 | custom fusion | flops 1572864 | bytes 7864832 | tf_op jit(solution)/shard_map/scatter | solution.py:1512
  580.6 4.5 pad_maximum_fusion.1.part_ref
  585.1 125.6 %shard_map.363 = (bf16[1920,1536]{1,0:T(8,128)(2,1)}, bf16[8,336,1536]{2,1,0:T(8,128)(2,1)}) custom-call(bf16[1920,1536]{1,0:T(8,128)(2,1)} %get-tuple-element.53.conv_ref, bf16[4,336,1536]{2,1,0:T(8,128)(2,1)} %pad_maximum_fusion.1.part_ref), custom_call_target="tpu_custom_call" | custom-call | tf_op jit(solution)/shard_map/pallas_call | solution.py:1261
  713.9 3.1 slice.169
  717.0 2.5 slice.162
  719.5 5.1 fusion.70
  727.7 6.0 copy.61
  733.7 1.9 copy.68
  735.7 2.3 copy.67
  739.1 8.9 %convert.42 = f32[5,384,1536]{2,1,0:T(8,128)} convert(bf16[5,384,1536]{2,1,0:T(8,128)(2,1)} %bitcast.132) | non-fusion elementwise | flops 2949120 | bytes 17694720 | tf_op jit(solution)/shard_map/reshape | solution.py:1519
  748.1 2.7 copy.89
  (163 shorter events, 34.4 us)
Async XLA Ops:
  7.2 20.7 %copy-start = (bf16[2048,384]{1,0:T(8,128)(2,1)S(1)}, bf16[2048,384]{1,0:T(8,128)(2,1)}, u32[]{:S(2)}) copy-start(bf16[2048,384]{1,0:T(8,128)(2,1)} %param.22) | copy-start | bytes 4718596
  7.2 573.4 %reduce-scatter.2.cloned.1.call-start = ((), (), s32[]{:S(2)}) async-start(), calls=%async_computation.1 | async-start | bytes 21233664 | tf_op jit(solution)/shard_map/reduce_scatter | solution.py:1368
  15.0 2.6 copy-start.27
  37.0 3.3 copy-start.22
  41.4 4.8 copy-start.24
  41.4 4.8 copy-start.39
  254.2 2.8 copy-start.7
  254.2 3.3 copy-start.28
  254.2 3.3 copy-start.36
  257.0 1.1 copy-start.30
  257.5 0.6 copy-start.33
  258.1 7.4 copy-start.21
  265.5 2.4 copy-start.19
  267.9 1.0 copy-start.23
  268.1 5.1 collective-permute-start
  271.4 1.8 copy-start.17
  278.7 19.1 %copy-start.8 = (f32[512,1536]{1,0:T(8,128)S(1)}, f32[512,1536]{1,0:T(8,128)}, u32[]{:S(2)}) copy-start(f32[512,1536]{1,0:T(8,128)} %get-tuple-element.38) | copy-start | bytes 9437188
  297.7 5.2 copy-start.5
  303.0 11.4 %copy-start.12 = (f32[512,1536]{1,0:T(8,128)}, f32[512,1536]{1,0:T(8,128)S(1)}, u32[]{:S(2)}) copy-start(f32[512,1536]{1,0:T(8,128)S(1)} %get-tuple-element.95) | copy-start | bytes 9437188
  303.0 0.7 copy-start.25
  303.0 0.8 copy-start.37
  303.5 0.9 copy-start.35
  304.4 10.0 %copy-start.2 = (bf16[512,1536]{1,0:T(8,128)(2,1)S(1)}, bf16[512,1536]{1,0:T(8,128)(2,1)}, u32[]{:S(2)}) copy-start(bf16[512,1536]{1,0:T(8,128)(2,1)} %get-tuple-element.42.refs_1_) | copy-start | bytes 4718596
  338.8 10.0 %copy-start.13 = (f32[512,1536]{1,0:T(8,128)S(1)}, f32[512,1536]{1,0:T(8,128)}, u32[]{:S(2)}) copy-start(f32[512,1536]{1,0:T(8,128)} %copy-done.12) | copy-start | bytes 9437188
  351.3 7.6 %copy-start.3 = (bf16[512,1536]{1,0:T(8,128)(2,1)}, bf16[512,1536]{1,0:T(8,128)(2,1)S(1)}, u32[]{:S(2)}) copy-start(bf16[512,1536]{1,0:T(8,128)(2,1)S(1)} %get-tuple-element.44.refs_1_) | copy-start | bytes 4718596
  387.8 14.7 %collective-permute-start.2 = (bf16[4,512,512]{2,1,0:T(8,128)(2,1)}, bf16[4,512,512]{2,1,0:T(8,128)(2,1)}, u32[]{:S(2)}, u32[]{:S(2)}) collective-permute-start(bf16[4,512,512]{2,1,0:T(8,128)(2,1)} %constant_dynamic-slice_fusion), channel_id=1, source_target_pairs={{0,4},{1,5},{2,6},{3,7},{4,0},{5,1},{6,2},{7,3},{8,12},{9,13},{10,... | collective-permute-start | bytes 6291464 | tf_op jit(solution)/shard_map/ppermute | solution.py:1349
  388.6 13.3 %copy-start.18 = (bf16[1536,192,1]{0,1,2:T(8,128)(2,1)S(1)}, bf16[1536,192,1]{0,1,2:T(8,128)(2,1)}, u32[]{:S(2)}) copy-start(bf16[1536,192,1]{0,1,2:T(8,128)(2,1)} %copy-done.17) | copy-start | bytes 1769476
  388.6 13.9 %copy-start.20 = (bf16[4,1024,512]{2,1,0:T(8,128)(2,1)S(1)}, bf16[4,1024,512]{2,1,0:T(8,128)(2,1)}, u32[]{:S(2)}) copy-start(bf16[4,1024,512]{2,1,0:T(8,128)(2,1)} %get-tuple-element.46) | copy-start | bytes 12582916
  399.8 165.2 %collective-permute-start.1 = (bf16[512,1536]{1,0:T(8,128)(2,1)}, bf16[512,1536]{1,0:T(8,128)(2,1)}, u32[]{:S(2)}, u32[]{:S(2)}) collective-permute-start(bf16[512,1536]{1,0:T(8,128)(2,1)} %fusion.40), channel_id=1, source_target_pairs={{0,0},{1,2},{2,4},{3,6},{4,1},{5,3},{6,5},{7,7},{8,8},{9,10},{10,1... | collective-permute-start | bytes 4718600 | tf_op jit(solution)/shard_map/ppermute | solution.py:1349
  402.4 2.8 copy-start.9
  402.4 2.7 copy-start.29
  402.5 2.7 copy-start.31
  402.5 2.7 copy-start.34
  415.7 3.2 copy-start.10
  415.7 4.4 copy-start.16
  420.1 4.2 copy-start.4
  420.1 4.2 copy-start.6
  435.6 120.1 %copy-start.14 = (bf16[2048,384]{1,0:T(8,128)(2,1)S(1)}, bf16[2048,384]{1,0:T(8,128)(2,1)}, u32[]{:S(2)}) copy-start(bf16[2048,384]{1,0:T(8,128)(2,1)} %gather_fusion) | copy-start | bytes 4718596
  435.6 120.1 %copy-start.26 = (f32[384]{0:T(512)S(1)}, f32[384]{0:T(512)}, u32[]{:S(2)}) copy-start(f32[384]{0:T(512)} %param.25) | copy-start | bytes 4612
  435.6 120.1 %copy-start.32 = (f32[384]{0:T(512)S(1)}, f32[384]{0:T(512)}, u32[]{:S(2)}) copy-start(f32[384]{0:T(512)} %param.26) | copy-start | bytes 4612
  555.7 10.9 %copy-start.15 = (f32[2,1024,384]{2,1,0:T(8,128)S(1)}, f32[2,1024,384]{2,1,0:T(8,128)}, u32[]{:S(2)}) copy-start(f32[2,1024,384]{2,1,0:T(8,128)} %get-tuple-element.52) | copy-start | bytes 9437188
  559.7 1.2 collective-permute-start.3
  561.0 2.5 collective-permute-start.4
  563.5 2.5 collective-permute-start.5
  566.6 2.4 copy-start.38
  713.9 5.6 copy-start.11
  739.1 11.6 %copy-start.1 = (bf16[2048,384]{1,0:T(8,128)(2,1)S(1)}, bf16[2048,384]{1,0:T(8,128)(2,1)}, u32[]{:S(2)}) copy-start(bf16[2048,384]{1,0:T(8,128)(2,1)} %param.22) | copy-start | bytes 4718596
Sparse Core Ops, SparseCore 0:
  338.9 125.7 reduce-scatter.1

commit v2 on v1

--- a/solution.py
+++ b/solution.py
@@ -289,7 +289,7 @@
 
 def front_kernel(
     chunk, taps, bits, total_rows,
-    rows_ref, gain_ref, bias_ref, w_ref, share_ref, small_ref, cot_ref,
+    rows_ref, affine_ref, w_ref, share_ref, small_ref, cot_ref,
     resid_ref, act_ref, stats_ref, small_out, cot_out, weights_ref,
     acc, rx_far, rx_near, rx_back, tx_far, tx_near, stage, rx_half, tx_stats, rx_stats,
     rx_far_step, rx_near_step, rx_back_step, tx_far_step, tx_near_step,
@@ -309,6 +309,7 @@
     reach = taps // 2
     count = length // chunk
     per_half = count // 2
+    assert count == 4
     tile = min(512, width)
     cut = width // 2
     mates = [mate_of(place, level, bit) for bit in range(bits)]
@@ -400,16 +401,22 @@
         for k in range(4):
             core_copy(z, k).wait_recv()
 
-    def weights_slot(t):
-        for lag, part in enumerate((weights_first, weights_second, weights_third, weights_fourth)):
-            if isinstance(t, int):
-                if lag <= t < 4 + lag:
-                    part(t - lag)
-                continue
-
-            @pl.when((t >= lag) & (t < 4 + lag))
-            def _(lag=lag, part=part):
-                part(t - lag)
+    stages = (weights_first, weights_second, weights_third, weights_fourth)
+    plans = (
+        (rank == 0, ((-1, 4, 4, 6), (4, 6, 7, 8), (5, 7, 8, 8), (8, 8, 8, 8))),
+        ((rank == 1) | (rank == 2), ((-1, 0, 0, 2), (1, 3, 4, 6), (3, 5, 6, 8), (5, 7, 8, 8))),
+        (rank == 3, ((-1, 3, 5, 7), (2, 6, 8, 8), (4, 7, 8, 8), (8, 8, 8, 8))),
+    )
+
+    def weights_turn(i):
+        for mine, plan in plans:
+            for stage, turns in zip(stages, plan):
+                for q, turn in enumerate(turns):
+                    if isinstance(i, int):
+                        if turn == i:
+                            pl.when(mine)(functools.partial(stage, q))
+                    elif 0 <= turn < 2 * count:
+                        pl.when(mine & (i == turn))(functools.partial(stage, q))
 
     own_copy = pltpu.make_async_copy(share_ref, piece(level, own), own_sem)
     own_copy.start()
@@ -440,14 +447,14 @@
         copy.start()
         copy.wait()
         sums = sums + rx_stats[bit]
-    weights_slot(0)
+    weights_first(0)
     mean = sums[0:1] / total_rows
     scale = lax.rsqrt(sums[1:2] / total_rows - mean * mean + EPSILON)
     stats_ref[...] = jnp.concatenate([mean, scale, jnp.zeros((6, own_cols), f32)], axis=0)
     row = lax.broadcasted_iota(jnp.int32, (length, own_cols), 0)
     for seq in range(seqs):
         centred = (rows_ref[seq].astype(f32) - mean) * scale
-        act = gelu(gain_ref[...] * centred + bias_ref[...])
+        act = gelu(affine_ref[0:1, :] * centred + affine_ref[1:2, :])
         for t in range(taps):
             moved = pltpu.roll(act, (reach - t) % length, 0) if t != reach else act
             inside = (row + (t - reach) >= 0) & (row + (t - reach) < length)
@@ -493,14 +500,7 @@
             swap_copy(c % per_half).start()
 
     def step(i, _):
-        @pl.when((rank == 0) & (i >= count))
-        def _():
-            weights_slot(i - count + 1)
-
-        @pl.when(((rank == 1) | (rank == 2)) & (i % 2 == 1))
-        def _():
-            weights_slot(i // 2 + 1)
-
+        weights_turn(i)
         c = i % count
         near = jnp.where(rank == 0, i < count, i >= count)
         seq = jnp.where(near, 1, 0)
@@ -570,12 +570,7 @@
         return 0
 
     lax.fori_loop(0, 2 * count, step, 0)
-    @pl.when(rank == 3)
-    def _():
-        lax.fori_loop(1, count + 1, lambda t, _: (weights_slot(t), 0)[1], 0)
-
-    for t in range(count + 1, 7):
-        weights_slot(t)
+    weights_turn(2 * count)
 
     @pl.when(rank >= 2)
     def _():
@@ -641,7 +636,7 @@
     return pl.BlockSpec(memory_space=pl.ANY)
 
 
-def front(rows, gain, bias, weight, share, small, cot, taps, bits, total_rows, chunk):
+def front(rows, affine, weight, share, small, cot, taps, bits, total_rows, chunk):
     seqs, length, own_cols = rows.shape
     depth, width = weight.shape
     levels = lax.axis_size("mp")
@@ -650,7 +645,7 @@
     shape = jax.ShapeDtypeStruct
     return pl.pallas_call(
         functools.partial(front_kernel, chunk, taps, bits, total_rows),
-        in_specs=[whole_spec()] * 6 + [any_spec()],
+        in_specs=[whole_spec()] * 5 + [any_spec()],
         out_specs=[whole_spec()] * 5 + [any_spec()],
         out_shape=[
             shape((half, width), f32),
@@ -708,7 +703,7 @@
         compiler_params=pltpu.CompilerParams(
             collective_id=0, has_side_effects=True, vmem_limit_bytes=56 << 20
         ),
-    )(rows, gain, bias, weight, share, small, cot)
+    )(rows, affine, weight, share, small, cot)
 
 
 def conv_back_kernel(
@@ -1368,15 +1363,34 @@
         value = lax.psum_scatter(value, "dp", scatter_dimension=0, axis_index_groups=inside)
         return value if cells == 1 else lax.psum(value, "dp", axis_index_groups=outside)
 
-    order = jnp.where(core == 0, row_order, row_order[::-1])
-    offsets = jnp.where(core == 0, jnp.array([0, length]), jnp.array([length, 0]))
-    source = (order + offsets[:, None].astype(jnp.int32)).reshape(group_rows)
+    order = row_order + length * jnp.arange(seq_count, dtype=jnp.int32)[:, None]
+    order = jnp.concatenate([order, order], axis=0)
+    source = lax.dynamic_slice_in_dim(order, core, seq_count, 0).reshape(group_rows)
     rows = block_input[source].reshape(seq_count, length, own_cols)
 
-    local = (w_inner.T, w_outer, w_out, jnp.concatenate([w_query.T, w_key.T, w_value.T], axis=0))
-    local_rows = sum(value.shape[0] for value in local)
-    share = lax.dynamic_slice_in_dim(
-        jnp.concatenate(local, axis=0), place % cell * (local_rows // cell), local_rows // cell, 0
+    local = ((w_inner, 1), (w_outer, 0), (w_out, 0), (w_query, 1), (w_key, 1), (w_value, 1))
+    local_rows = sum(value.shape[axis] for value, axis in local)
+    share_rows = local_rows // cell
+
+    def share_of(p):
+        first, last, at, parts = p * share_rows, (p + 1) * share_rows, 0, []
+        for k, (value, axis) in enumerate(local):
+            low, high = max(first - at, 0), min(last - at, value.shape[axis])
+            at += value.shape[axis]
+            if low < high:
+                parts.append((k, axis, low, high))
+
+        def build(*values):
+            found = []
+            for k, axis, low, high in parts:
+                part = lax.slice_in_dim(values[k], low, high, axis=axis)
+                found.append(part.T if axis else part)
+            return jnp.concatenate(found, axis=0)
+
+        return build
+
+    share = lax.switch(
+        place % cell, [share_of(p) for p in range(cell)], *(value for value, _ in local)
     )
     small = jnp.concatenate(
         [
@@ -1390,8 +1404,7 @@
     conv_flat = conv_weight.reshape(taps * own_cols, width)
     resid_one, act_taps, stats, small, cot, weights = front(
         rows,
-        batch_gain[None],
-        batch_bias[None],
+        jnp.stack([batch_gain, batch_bias]),
         conv_flat,
         share,
         small,

time: 767 us -> 706 us (0.920)
  Pallas kernels: 523 us -> 485 us
  local copies, waits for them, and re-layouts: 80 us -> 58.5 us
    pallas_call x1, Pallas kernels: 207 us -> 169 us  [front(): pl.pallas_call(functools.partial(front_kernel, chunk, taps, bits, total_r...]
    unnamed x100 -> x89, local copies, waits for them, and re-layouts: 31.6 us -> 14.8 us
  transfers between devices with their start and end apart: 7 -> 7, of which waited for: 3 -> 3; matrix products, arithmetic and copies ran while one was open for 10% -> 11% of each run, Pallas kernels for 21% -> 22%
where the time goes in v2:
time: 706 us; the launch traced here: 698 us
  Pallas kernels  485 us (69%)
  matrix products  73.4 us (10%)
  local copies, waits for them, and re-layouts  58.5 us (8%)
  other arithmetic  57.5 us (8%)
  between operations  15 us (2%)
    pallas_call x1, Pallas kernels, front(): pl.pallas_call(functools.partial(front_kernel, chunk, taps, bits, total_r...  169 us
    pallas_call x1, Pallas kernels, last_sums(): pl.pallas_call(last_sums_kernel, in_specs=[whole_spec()] * 2, out_specs=[...  125 us
    pallas_call x1, Pallas kernels, conv_back(): pl.pallas_call(functools.partial(conv_back_kernel, chunk, taps), in_specs...  120 us
    pallas_call x1, Pallas kernels, attend_back(): pl.pallas_call(functools.partial(attend_back_kernel, dk, dv, bq, scale),...  25.5 us
    pallas_call x2, Pallas kernels, weight_grads(): pl.pallas_call(functools.partial(weight_grads_kernel, cell, len(pairs)),...  25.5 us
    pallas_call x1, Pallas kernels, attend(): pl.pallas_call(functools.partial(attend_kernel, dk, dv, bq), grid=(groups...  19 us
    unnamed x89, local copies, waits for them, and re-layouts  14.8 us
  transfers between devices with their start and end apart: 7, of which 3 were waited for; matrix products, arithmetic and copies ran while one was open for 11% of the time, Pallas kernels for 22%

profile of v2, /device:TPU:9, one launch (start us, length us, event | category | flops | bytes accessed | tf_op | source)
XLA Modules:
  0.0 698.1 jit_solution(17202919224584030874)
XLA Ops:
  13.1 9.1 %gather_fusion = bf16[2048,384]{1,0:T(8,128)(2,1)} fusion(bf16[2048,384]{1,0:T(8,128)(2,1)S(1)} %copy-done, s32[2048]{0:T(1024)S(1)} %broadcast_clamp_fusion), kind=kCustom, calls=%fused_computation | custom fusion | bytes 3153920 | tf_op jit(solution)/shard_map/gather | solution.py:1369
  22.9 2.7 conditional.1
  22.9 1.9 slice_bitcast_fusion.1
  25.6 169.4 %shard_map.356 = (f32[512,1536]{1,0:T(8,128)}, bf16[2,1024,1920]{2,1,0:T(8,128)(2,1)}, f32[8,384]{1,0:T(8,128)}, f32[4,200,128]{2,1,0:T(8,128)}, bf16[512,1536]{...) custom-call(bf16[2,1024,384]{2,1,0:T(8,128)(2,1)} %bitcast.133, f32[2,384]{1,0:T(2,128)} %pad_maximum_fusion.7.affine_ref, ...), custom_call_target="tpu_custom_call" | custom-call | flops 12079595520 | bytes 419430400 | tf_op jit(solution)/shard_map/pallas_call | solution.py:646
  195.0 2.3 reduce_sum.135
  198.9 7.3 %fusion.46 = f32[4,512,640]{2,1,0:T(8,128)S(1)} fusion(bf16[4,2560,1536]{2,1,0:T(8,128)(2,1)} %get-tuple-element.74, bf16[512,1536]{1,0:T(8,128)(2,1)S(1)} %add_convert_fusion.3.refs_3_), kind=kOutput, calls=%fused_computation.69 | convolution fusion | flops 4026531840 | bytes 14680064 | tf_op jit(solution)/shard_map/rd,znd->zrn/dot_general | solution.py:1436
  206.3 2.3 copy-done.20
  210.4 1.4 add_convert_fusion.4
  212.2 1.8 fusion.43.rel_ref
  214.0 3.2 broadcast_select_fusion.1
  217.2 2.3 pad_maximum_fusion.3.kv_ref
  219.5 19.0 %shard_map.357 = (bf16[4,512,384]{2,1,0:T(8,128)(2,1)S(1)}, bf16[4,2,512,1024]{3,2,1,0:T(8,128)(2,1)}) custom-call(bf16[4,512,128]{2,1,0:T(8,128)(2,1)S(1)} %get-tuple-element.127.qw_ref, bf16[4,512,128]{2,1,0:T(8,128)(2,1)S(1)} %get-tuple-element.126.qr_ref, bf16[4,1024,512]{2,1,0:T(8,128)(2,1)} %pad_maximum_fusion.3.kv_ref, ...), custom_call_target="tpu_custom_call" | custom-call | tf_op jit(solution)/shard_map/pallas_call | solution.py:94
  238.5 5.2 fusion.78
  245.2 9.9 %fusion.13 = (bf16[4,512,768]{2,1,0:T(8,128)(2,1)}, f32[4,768,512]{1,2,0:T(8,128)S(1)}) fusion(f32[4,768]{1,0:T(4,128)S(1)} %bitcast.151, bf16[512,1536]{1,0:T(8,128)(2,1)S(1)} %add_convert_fusion.2.refs_3_, bf16[4,2560,1536]{2,1,0:T(8,128)(2,1)} %get-tuple-element.74), kind=kOutput, calls=%fused_computation.26 | convolution fusion | flops 4842848256 | bytes 20459520 | tf_op jit(solution)/shard_map/rd,znd->zrn/dot_general | solution.py:1453
  255.1 10.2 %fusion.79 = (bf16[4,768]{1,0:T(4,128)(2,1)S(1)}, bf16[4,512,768]{2,1,0:T(8,128)(2,1)}) fusion(f32[4,768,512]{1,2,0:T(8,128)S(1)} %get-tuple-element.147, f32[4,768]{1,0:T(4,128)S(1)} %bitcast.152, bf16[512,1536]{1,0:T(8,128)(2,1)S(1)} %copy-done.2, bf16[4,2560,1536]{2,1,0:T(8,128)(2,1)} %get-tuple-element.74), kind=kOutput, calls=%fused_computation.141 | convolution fusion | flops 4850709504 | bytes 20465664 | tf_op jit(solution)/shard_map/rd,znd->zrn/dot_general | solution.py:1464
  265.3 14.2 %shard_map.358 = bf16[8,4,192,1536]{3,2,1,0:T(8,128)(2,1)} custom-call(bf16[4,512,768]{2,1,0:T(8,128)(2,1)} %get-tuple-element.146.refs_0_, bf16[512,1536]{1,0:T(8,128)(2,1)S(1)} %copy-done.2, bf16[4,512,768]{2,1,0:T(8,128)(2,1)} %get-tuple-element.151.refs_2_, bf16[512,1536]{1,0:T(8,128)(2,1)S(1)} %add_convert_fusion.2.refs_3_), custom_call_target="tpu_custom_call" | custom-call | flops 9663676416 | bytes 31457280 | tf_op jit(solution)/shard_map/pallas_call | solution.py:1036
  279.5 9.9 %multiply_reduce_fusion.1 = (bf16[1536]{0:T(1024)(128)(2,1)S(1)}, f32[512]{0:T(512)S(1)}, f32[512]{0:T(512)S(1)}, bf16[1536]{0:T(1024)(128)(2,1)S(1)}, f32[512,1536]{1,0:T(8,128)S(1)}) fusion(f32[512,1536]{1,0:T(8,128)} %copy-done.12, f32[512]{0:T(512)S(1)} %add_rsqrt_fusion, f32[512]{0:T(512)S(1)} %broadcast_multiply_fusion.5, f32[1536]{0:T(1024)S(1)} %copy-done.25, ...), kind=kOutput, calls=%fused_computation.51 | convolution fusion | flops 4838912000 | bytes 18894848 | tf_op jit(solution)/shard_map/zrn,znd->rd/dot_general | solution.py:1468
  289.5 2.6 fusion.71
  292.1 7.6 %fusion.57.dmix_ref = bf16[4,512,384]{2,1,0:T(8,128)(2,1)} fusion(bf16[512,1536]{1,0:T(8,128)(2,1)S(1)} %get-tuple-element.79.refs_1_, bf16[4,2560,1536]{2,1,0:T(8,128)(2,1)} %get-tuple-element.74), kind=kOutput, calls=%fused_computation.80 | convolution fusion | flops 2416705536 | bytes 7864320 | tf_op jit(solution)/shard_map/rd,znd->zrn/dot_general | solution.py:1476
  299.7 25.5 %shard_map.359 = (bf16[4,512,128]{2,1,0:T(8,128)(2,1)S(1)}, f32[4,8,128]{2,1,0:T(8,128)S(1)}, bf16[4,1024,512]{2,1,0:T(8,128)(2,1)}, bf16[4,1536,128]{2,1,0:T(8,128)(2,1)S(1)}) custom-call(bf16[4,512,128]{2,1,0:T(8,128)(2,1)S(1)} %get-tuple-element.127.qw_ref, bf16[4,512,128]{2,1,0:T(8,128)(2,1)S(1)} %get-tuple-element.126.qr_ref, ...), custom_call_target="tpu_custom_call" | custom-call | tf_op jit(solution)/shard_map/pallas_call | solution.py:179
  325.3 3.0 constant_dynamic-slice_fusion
  329.2 11.2 %fusion.40 = bf16[512,1536]{1,0:T(8,128)(2,1)} fusion(f32[512,1536]{1,0:T(8,128)} %copy-done.12, bf16[4,512,768]{2,1,0:T(8,128)(2,1)} %get-tuple-element.146.refs_0_, bf16[4,2560,1536]{2,1,0:T(8,128)(2,1)} %get-tuple-element.74), kind=kOutput, calls=%fused_computation.62 | convolution fusion | flops 4833411072 | bytes 17301504 | tf_op jit(solution)/shard_map/zrn,znd->rd/dot_general | solution.py:1458
  340.4 2.3 collective-permute-start.1
  343.3 2.5 add_convert_fusion
  346.0 9.7 %multiply_reduce_fusion.2 = (bf16[1536]{0:T(1024)(128)(2,1)S(1)}, f32[512]{0:T(512)S(1)}, f32[512]{0:T(512)S(1)}, bf16[1536]{0:T(1024)(128)(2,1)S(1)}, f32[512,1536]{1,0:T(8,128)}) fusion(f32[512,1536]{1,0:T(8,128)S(1)} %copy-done.9, f32[512]{0:T(512)S(1)} %copy-done.34, f32[512]{0:T(512)S(1)} %copy-done.31, f32[1536]{0:T(1024)S(1)} %copy-done.29, ...), kind=kOutput, calls=%fused_computation.52 | convolution fusion | flops 4038848512 | bytes 16797696 | tf_op jit(solution)/shard_map/zrn,znd->rd/dot_general | solution.py:1485
  356.5 1.4 pad.11.refs_4_
  357.9 1.8 pad_maximum_fusion.5.refs_2_
  359.6 1.2 copy-done.17
  360.9 4.2 add_convert_fusion.1.grad_ref
  365.1 11.2 %shard_map.360 = bf16[8,4,144,1536]{3,2,1,0:T(8,128)(2,1)} custom-call(bf16[4,512,384]{2,1,0:T(8,128)(2,1)S(1)} %copy-done.6, bf16[512,1536]{1,0:T(8,128)(2,1)S(1)} %copy-done.4, bf16[4,512,640]{2,1,0:T(8,128)(2,1)} %pad_maximum_fusion.5.refs_2_, bf16[512,1536]{1,0:T(8,128)(2,1)} %copy-done.23, bf16[8,4,16,1536]{3,2,1,0:T(8,128)(2,1)} %pad.11.refs_4_), custom_call_target="tpu_custom_call" | custom-call | flops 6442450944 | bytes 31457280 | tf_op jit(solution)/shard_map/pallas_call | solution.py:1036
  376.4 120.0 %shard_map.361 = (f32[2,1024,384]{2,1,0:T(8,128)}, bf16[2,1024,384]{2,1,0:T(8,128)(2,1)}, bf16[1920,1536]{1,0:T(8,128)(2,1)}, bf16[4,144,1536]{2,1,0:T(8,128)(2,1)}, bf16[4,2,2,144,1536]{4,3,2,1,0:T(8,128)(2,1)}) custom-call(bf16[512,1536]{1,0:T(8,128)(2,1)} %add_convert_fusion.1.grad_ref, bf16[2,1024,1920]{2,1,0:T(8,128)(2,1)} %get-tuple-element.82.act_ref, ...), custom_call_target="tpu_custom_call" | custom-call | tf_op jit(solution)/shard_map/pallas_call | solution.py:960
  496.4 4.0 multiply_reduce_fusion
  500.5 1.1 collective-permute-done.3
  502.3 1.9 collective-permute-done.4
  504.8 1.9 collective-permute-done.5
  507.3 2.4 fusion.39
  509.8 11.5 %scatter_custom_fusion = f32[2048,384]{1,0:T(8,128)} fusion(s32[2048]{0:T(1024)} %bitcast.149, f32[2048,384]{1,0:T(8,128)S(1)} %fusion.39, bf16[2048,384]{1,0:T(8,128)(2,1)} %bitcast.143, f32[]{:T(128)} %constant.72.clone.1), kind=kCustom, calls=%fused_computation.43 | custom fusion | flops 1572864 | bytes 7864832 | tf_op jit(solution)/shard_map/scatter | solution.py:1525
  521.3 4.5 pad_maximum_fusion.4.part_ref
  525.8 125.2 %shard_map.362 = (bf16[1920,1536]{1,0:T(8,128)(2,1)}, bf16[8,336,1536]{2,1,0:T(8,128)(2,1)}) custom-call(bf16[1920,1536]{1,0:T(8,128)(2,1)} %get-tuple-element.88.conv_ref, bf16[4,336,1536]{2,1,0:T(8,128)(2,1)} %pad_maximum_fusion.4.part_ref), custom_call_target="tpu_custom_call" | custom-call | tf_op jit(solution)/shard_map/pallas_call | solution.py:1256
  654.2 3.1 slice.204
  657.4 2.5 slice.197
  659.9 5.1 fusion.72
  666.7 1.3 fusion.75
  668.1 6.0 copy.65
  674.1 1.9 copy.82
  676.0 2.3 copy.81
  679.5 8.9 %convert.42 = f32[5,384,1536]{2,1,0:T(8,128)} convert(bf16[5,384,1536]{2,1,0:T(8,128)(2,1)} %bitcast.136) | non-fusion elementwise | flops 2949120 | bytes 17694720 | tf_op jit(solution)/shard_map/reshape | solution.py:1532
  688.4 2.7 copy.106
  (154 shorter events, 22.5 us)
Async XLA Ops:
  7.2 5.9 copy-start
  7.2 514.1 %reduce-scatter.2.cloned.1.call-start = ((), (), s32[]{:S(2)}) async-start(), calls=%async_computation.1 | async-start | bytes 21233664 | tf_op jit(solution)/shard_map/reduce_scatter | solution.py:1363
  11.1 0.6 copy-start.27
  13.1 9.1 %copy-start.21 = (bf16[384,1536]{1,0:T(8,128)(2,1)S(1)}, bf16[384,1536]{1,0:T(8,128)(2,1)}, u32[]{:S(2)}) copy-start(bf16[384,1536]{1,0:T(8,128)(2,1)} %param.41) | copy-start | bytes 3538948
  13.1 9.1 %copy-start.39 = (f32[768]{0:T(1024)S(1)}, f32[768]{0:T(1024)}, u32[]{:S(2)}) copy-start(f32[768]{0:T(1024)} %param.45) | copy-start | bytes 9220
  195.0 2.8 copy-start.7
  195.0 3.3 copy-start.28
  195.0 3.3 copy-start.36
  197.8 1.1 copy-start.30
  198.3 0.6 copy-start.33
  198.9 7.3 %copy-start.23 = (bf16[512,1536]{1,0:T(8,128)(2,1)}, bf16[512,1536]{1,0:T(8,128)(2,1)S(1)}, u32[]{:S(2)}) copy-start(bf16[512,1536]{1,0:T(8,128)(2,1)S(1)} %add_convert_fusion.3.refs_3_) | copy-start | bytes 4718596
  206.3 2.4 copy-start.20
  208.6 1.0 copy-start.24
  208.9 5.1 collective-permute-start
  212.2 1.8 copy-start.18
  219.5 19.1 %copy-start.8 = (f32[512,1536]{1,0:T(8,128)S(1)}, f32[512,1536]{1,0:T(8,128)}, u32[]{:S(2)}) copy-start(f32[512,1536]{1,0:T(8,128)} %get-tuple-element.73) | copy-start | bytes 9437188
  238.5 5.2 copy-start.5
  243.8 11.3 %copy-start.12 = (f32[512,1536]{1,0:T(8,128)}, f32[512,1536]{1,0:T(8,128)S(1)}, u32[]{:S(2)}) copy-start(f32[512,1536]{1,0:T(8,128)S(1)} %get-tuple-element.145) | copy-start | bytes 9437188
  243.8 0.7 copy-start.25
  243.8 0.8 copy-start.37
  244.3 0.9 copy-start.35
  245.2 9.9 %copy-start.2 = (bf16[512,1536]{1,0:T(8,128)(2,1)S(1)}, bf16[512,1536]{1,0:T(8,128)(2,1)}, u32[]{:S(2)}) copy-start(bf16[512,1536]{1,0:T(8,128)(2,1)} %get-tuple-element.77.refs_1_) | copy-start | bytes 4718596
  279.5 10.0 %copy-start.13 = (f32[512,1536]{1,0:T(8,128)S(1)}, f32[512,1536]{1,0:T(8,128)}, u32[]{:S(2)}) copy-start(f32[512,1536]{1,0:T(8,128)} %copy-done.12) | copy-start | bytes 9437188
  292.1 7.6 %copy-start.3 = (bf16[512,1536]{1,0:T(8,128)(2,1)}, bf16[512,1536]{1,0:T(8,128)(2,1)S(1)}, u32[]{:S(2)}) copy-start(bf16[512,1536]{1,0:T(8,128)(2,1)S(1)} %get-tuple-element.79.refs_1_) | copy-start | bytes 4718596
  328.3 15.0 %collective-permute-start.2 = (bf16[4,512,512]{2,1,0:T(8,128)(2,1)}, bf16[4,512,512]{2,1,0:T(8,128)(2,1)}, u32[]{:S(2)}, u32[]{:S(2)}) collective-permute-start(bf16[4,512,512]{2,1,0:T(8,128)(2,1)} %constant_dynamic-slice_fusion), channel_id=1, source_target_pairs={{0,4},{1,5},{2,6},{3,7},{4,0},{5,1},{6,2},{7,3},{8,12},{9,13},{10,... | collective-permute-start | bytes 6291464 | tf_op jit(solution)/shard_map/ppermute | solution.py:1344
  329.2 13.6 %copy-start.19 = (bf16[1536,192,1]{0,1,2:T(8,128)(2,1)S(1)}, bf16[1536,192,1]{0,1,2:T(8,128)(2,1)}, u32[]{:S(2)}) copy-start(bf16[1536,192,1]{0,1,2:T(8,128)(2,1)} %copy-done.18) | copy-start | bytes 1769476
  329.2 14.1 %copy-start.22 = (bf16[4,1024,512]{2,1,0:T(8,128)(2,1)S(1)}, bf16[4,1024,512]{2,1,0:T(8,128)(2,1)}, u32[]{:S(2)}) copy-start(bf16[4,1024,512]{2,1,0:T(8,128)(2,1)} %get-tuple-element.81) | copy-start | bytes 12582916
  340.4 164.4 %collective-permute-start.1 = (bf16[512,1536]{1,0:T(8,128)(2,1)}, bf16[512,1536]{1,0:T(8,128)(2,1)}, u32[]{:S(2)}, u32[]{:S(2)}) collective-permute-start(bf16[512,1536]{1,0:T(8,128)(2,1)} %fusion.40), channel_id=1, source_target_pairs={{0,0},{1,2},{2,4},{3,6},{4,1},{5,3},{6,5},{7,7},{8,8},{9,10},{10,1... | collective-permute-start | bytes 4718600 | tf_op jit(solution)/shard_map/ppermute | solution.py:1344
  343.2 2.7 copy-start.9
  343.2 2.7 copy-start.29
  343.3 2.7 copy-start.31
  343.3 2.7 copy-start.34
  356.5 3.2 copy-start.10
  356.5 4.4 copy-start.17
  360.9 4.2 copy-start.4
  360.9 4.2 copy-start.6
  376.4 120.0 %copy-start.15 = (bf16[2048,384]{1,0:T(8,128)(2,1)S(1)}, bf16[2048,384]{1,0:T(8,128)(2,1)}, u32[]{:S(2)}) copy-start(bf16[2048,384]{1,0:T(8,128)(2,1)} %gather_fusion) | copy-start | bytes 4718596
  376.4 120.1 %copy-start.26 = (f32[384]{0:T(512)S(1)}, f32[384]{0:T(512)}, u32[]{:S(2)}) copy-start(f32[384]{0:T(512)} %param.31) | copy-start | bytes 4612
  376.4 120.1 %copy-start.32 = (f32[384]{0:T(512)S(1)}, f32[384]{0:T(512)}, u32[]{:S(2)}) copy-start(f32[384]{0:T(512)} %param.32) | copy-start | bytes 4612
  496.4 10.9 %copy-start.16 = (f32[2,1024,384]{2,1,0:T(8,128)S(1)}, f32[2,1024,384]{2,1,0:T(8,128)}, u32[]{:S(2)}) copy-start(f32[2,1024,384]{2,1,0:T(8,128)} %get-tuple-element.87) | copy-start | bytes 9437188
  500.5 1.2 collective-permute-start.3
  501.7 2.5 collective-permute-start.4
  504.2 2.5 collective-permute-start.5
  507.3 2.4 copy-start.38
  654.2 5.6 copy-start.11
  679.5 11.6 %copy-start.1 = (bf16[2048,384]{1,0:T(8,128)(2,1)S(1)}, bf16[2048,384]{1,0:T(8,128)(2,1)}, u32[]{:S(2)}) copy-start(bf16[2048,384]{1,0:T(8,128)(2,1)} %param.28) | copy-start | bytes 4718596
Sparse Core Ops, SparseCore 0:
  279.6 126.2 reduce-scatter.1

commit v3 on v2

--- a/solution.py
+++ b/solution.py
@@ -1291,6 +1291,71 @@
     )(conv, parts)
 
 
+def give_kernel(
+    cuts, conv_ref, part_ref,
+    conv_out, outer_out, inner_out, out_out, query_out, key_out, value_out, rest_out,
+    inner_rows, qkv_rows,
+):
+    p = pl.program_id(0)
+    cell = pl.num_programs(0)
+    conv_out[...] = conv_ref[...].astype(f32)
+    a, b, c, d = cuts[0], cuts[0] + cuts[1], sum(cuts[:3]), sum(cuts)
+    outer_out[...] = part_ref[0, :a].astype(f32)
+    inner_rows[pl.ds(pl.multiple_of(p * cuts[1], 16), cuts[1])] = part_ref[0, a:b]
+    out_out[...] = part_ref[0, b:c].astype(f32)
+    qkv_rows[pl.ds(pl.multiple_of(p * cuts[3], 16), cuts[3])] = part_ref[0, c:d]
+    rest_out[0] = part_ref[0, d:].astype(f32)
+
+    @pl.when(p == cell - 1)
+    def _():
+        inner_out[...] = inner_rows[...].astype(f32).T
+        at = 0
+        for out in (query_out, key_out, value_out):
+            size = out.shape[1]
+            out[...] = qkv_rows[at : at + size].astype(f32).T
+            at += size
+
+
+def give(conv, parts, cuts, qcols, vcols):
+    rows, width = conv.shape
+    cell, share, _ = parts.shape
+    rest = share - sum(cuts)
+    shape = jax.ShapeDtypeStruct
+    by_rows = lambda size: pl.BlockSpec((size, width), lambda p: (p, 0))
+    fixed = lambda cols: pl.BlockSpec((width, cols), lambda p: (0, 0))
+    inner_cols = cell * cuts[1]
+    return pl.pallas_call(
+        functools.partial(give_kernel, cuts),
+        grid=(cell,),
+        in_specs=[by_rows(rows // cell), block_spec(share, width)],
+        out_specs=[
+            by_rows(rows // cell),
+            by_rows(cuts[0]),
+            fixed(inner_cols),
+            by_rows(cuts[2]),
+            fixed(qcols),
+            fixed(qcols),
+            fixed(vcols),
+            block_spec(rest, width),
+        ],
+        out_shape=[
+            shape((rows, width), f32),
+            shape((cell * cuts[0], width), f32),
+            shape((width, inner_cols), f32),
+            shape((cell * cuts[2], width), f32),
+            shape((width, qcols), f32),
+            shape((width, qcols), f32),
+            shape((width, vcols), f32),
+            shape((cell, rest, width), f32),
+        ],
+        scratch_shapes=[
+            pltpu.VMEM((inner_cols, width), bf16),
+            pltpu.VMEM((cell * cuts[3], width), bf16),
+        ],
+        compiler_params=pltpu.CompilerParams(vmem_limit_bytes=50 << 20),
+    )(conv, parts)
+
+
 def on_device(
     block_input,
     row_order,
@@ -1529,14 +1594,14 @@
         g_conv = lax.psum(g_conv, "dp", axis_index_groups=outside)
     parts = jnp.concatenate([feed_parts, attend_parts], axis=1)
     g_conv, whole = last_sums(g_conv, parts)
-    g_conv = g_conv.astype(f32).reshape(taps, own_cols, width)
-    whole = whole.astype(f32)
-    sums, at = [], 0
-    for cols in (hidden_cols, hidden_cols, vcols, 2 * qcols + vcols):
-        sums.append(whole[:, at : at + cols // cell].reshape(cols, width))
-        at += cols // cell
-    g_outer, g_inner, g_out, g_qkv = sums
-    rest = whole[:, at : at + extra_rows].reshape(-1)[:used]
+    cuts = tuple(
+        cols // cell for cols in (hidden_cols, hidden_cols, vcols, 2 * qcols + vcols)
+    )
+    g_conv, g_outer, g_inner, g_out, g_query, g_key, g_value, rest = give(
+        g_conv, whole, cuts, qcols, vcols
+    )
+    g_conv = g_conv.reshape(taps, own_cols, width)
+    rest = rest[:, :extra_rows].reshape(-1)[:used]
 
     def take(start, size):
         return rest[start : start + size]
@@ -1552,16 +1617,16 @@
         g_batch_bias,
         take(0, width),
         take(width, width),
-        g_qkv[:qcols].T,
-        g_qkv[qcols : 2 * qcols].T,
-        g_qkv[2 * qcols :].T,
+        g_query,
+        g_key,
+        g_value,
         take(base, rel_size).reshape(features, qcols),
         take(base + rel_size, qcols).reshape(pair, dk),
         take(base + rel_size + qcols, qcols).reshape(pair, dk),
         g_out,
         take(2 * width, width),
         take(3 * width, width),
-        g_inner.T,
+        g_inner,
         take(base + rel_size + 2 * qcols, hidden_cols),
         g_outer,
     )

time: 706 us -> 690 us (0.977)
  local copies, waits for them, and re-layouts: 58.5 us -> 32.1 us
  Pallas kernels: 485 us -> 502 us
  other arithmetic: 57.5 us -> 48.5 us
    pallas_call x0 -> x1, Pallas kernels: none -> 17.3 us  [give(): pl.pallas_call(functools.partial(give_kernel, cuts), grid=(cell,), in_spe...]
    slice x6 -> x1, local copies, waits for them, and re-layouts: 12.8 us -> 0.03 us  [on_device(): rest = rest[:, :extra_rows].reshape(-1)[:used]]
    reshape x1 -> x0, other arithmetic: 8.94 us -> none  [on_device(): g_conv = g_conv.astype(f32).reshape(taps, own_cols, width)]
    unnamed x89 -> x82, local copies, waits for them, and re-layouts: 14.8 us -> 6.41 us
  transfers between devices with their start and end apart: 7 -> 7, of which waited for: 3 -> 3; matrix products, arithmetic and copies ran while one was open for 11% -> 12% of each run, Pallas kernels for 22% -> 23%
where the time goes in v3:
time: 690 us; the launch traced here: 683 us
  Pallas kernels  502 us (73%)
  matrix products  75.8 us (11%)
  other arithmetic  48.5 us (7%)
  local copies, waits for them, and re-layouts  32.1 us (5%)
  between operations  15 us (2%)
    pallas_call x1, Pallas kernels, front(): pl.pallas_call(functools.partial(front_kernel, chunk, taps, bits, total_r...  169 us
    pallas_call x1, Pallas kernels, last_sums(): pl.pallas_call(last_sums_kernel, in_specs=[whole_spec()] * 2, out_specs=[...  125 us
    pallas_call x1, Pallas kernels, conv_back(): pl.pallas_call(functools.partial(conv_back_kernel, chunk, taps), in_specs...  120 us
    pallas_call x1, Pallas kernels, attend_back(): pl.pallas_call(functools.partial(attend_back_kernel, dk, dv, bq, scale),...  25.6 us
    pallas_call x2, Pallas kernels, weight_grads(): pl.pallas_call(functools.partial(weight_grads_kernel, cell, len(pairs)),...  25.4 us
    pallas_call x1, Pallas kernels, attend(): pl.pallas_call(functools.partial(attend_kernel, dk, dv, bq), grid=(groups...  19 us
    pallas_call x1, Pallas kernels, give(): pl.pallas_call(functools.partial(give_kernel, cuts), grid=(cell,), in_spe...  17.3 us
  transfers between devices with their start and end apart: 7, of which 3 were waited for; matrix products, arithmetic and copies ran while one was open for 12% of the time, Pallas kernels for 23%

profile of v3, /device:TPU:9, one launch (start us, length us, event | category | flops | bytes accessed | tf_op | source)
XLA Modules:
  0.0 682.6 jit_solution(4598320851047990763)
XLA Ops:
  7.3 0.9 reshape.235
  8.2 0.8 reshape.236
  10.3 0.8 broadcast_add_fusion
  11.7 0.8 convert_element_type.78
  13.1 9.1 %gather_fusion = bf16[2048,384]{1,0:T(8,128)(2,1)} fusion(bf16[2048,384]{1,0:T(8,128)(2,1)S(1)} %copy-done, s32[2048]{0:T(1024)S(1)} %broadcast_clamp_fusion), kind=kCustom, calls=%fused_computation | custom fusion | bytes 3153920 | tf_op jit(solution)/shard_map/gather | solution.py:1434
  22.9 2.7 conditional.1
  22.9 1.9 slice_bitcast_fusion.1
  25.6 169.4 %shard_map.356 = (f32[512,1536]{1,0:T(8,128)}, bf16[2,1024,1920]{2,1,0:T(8,128)(2,1)}, f32[8,384]{1,0:T(8,128)}, f32[4,200,128]{2,1,0:T(8,128)}, bf16[512,1536]{...) custom-call(bf16[2,1024,384]{2,1,0:T(8,128)(2,1)} %bitcast.121, f32[2,384]{1,0:T(2,128)} %pad_maximum_fusion.7.affine_ref, ...), custom_call_target="tpu_custom_call" | custom-call | flops 12079595520 | bytes 419430400 | tf_op jit(solution)/shard_map/pallas_call | solution.py:646
  195.0 2.3 reduce_sum.135
  198.9 9.8 %fusion.46 = f32[4,512,640]{2,1,0:T(8,128)} fusion(bf16[4,2560,1536]{2,1,0:T(8,128)(2,1)} %get-tuple-element.82, bf16[512,1536]{1,0:T(8,128)(2,1)S(1)} %add_convert_fusion.3.refs_3_), kind=kOutput, calls=%fused_computation.69 | convolution fusion | flops 4026531840 | bytes 14680064 | tf_op jit(solution)/shard_map/rd,znd->zrn/dot_general | solution.py:1501
  208.8 2.5 slice.231
  212.1 1.4 add_convert_fusion.4
  213.9 1.8 fusion.43.rel_ref
  215.8 3.2 broadcast_select_fusion.1
  219.0 2.3 pad_maximum_fusion.3.kv_ref
  221.2 19.0 %shard_map.357 = (bf16[4,512,384]{2,1,0:T(8,128)(2,1)S(1)}, bf16[4,2,512,1024]{3,2,1,0:T(8,128)(2,1)}) custom-call(bf16[4,512,128]{2,1,0:T(8,128)(2,1)S(1)} %get-tuple-element.141.qw_ref, bf16[4,512,128]{2,1,0:T(8,128)(2,1)S(1)} %get-tuple-element.140.qr_ref, bf16[4,1024,512]{2,1,0:T(8,128)(2,1)} %pad_maximum_fusion.3.kv_ref, ...), custom_call_target="tpu_custom_call" | custom-call | tf_op jit(solution)/shard_map/pallas_call | solution.py:94
  240.3 5.2 fusion.76
  246.9 9.9 %fusion.13 = (bf16[4,512,768]{2,1,0:T(8,128)(2,1)}, f32[4,768,512]{1,2,0:T(8,128)S(1)}) fusion(f32[4,768]{1,0:T(4,128)S(1)} %bitcast.132, bf16[512,1536]{1,0:T(8,128)(2,1)S(1)} %add_convert_fusion.2.refs_3_, bf16[4,2560,1536]{2,1,0:T(8,128)(2,1)} %get-tuple-element.82), kind=kOutput, calls=%fused_computation.26 | convolution fusion | flops 4842848256 | bytes 20459520 | tf_op jit(solution)/shard_map/rd,znd->zrn/dot_general | solution.py:1518
  256.8 10.2 %fusion.77 = (bf16[4,768]{1,0:T(4,128)(2,1)S(1)}, bf16[4,512,768]{2,1,0:T(8,128)(2,1)}) fusion(f32[4,768,512]{1,2,0:T(8,128)S(1)} %get-tuple-element.159, f32[4,768]{1,0:T(4,128)S(1)} %bitcast.133, bf16[512,1536]{1,0:T(8,128)(2,1)S(1)} %copy-done.2, bf16[4,2560,1536]{2,1,0:T(8,128)(2,1)} %get-tuple-element.82), kind=kOutput, calls=%fused_computation.139 | convolution fusion | flops 4850709504 | bytes 20465664 | tf_op jit(solution)/shard_map/rd,znd->zrn/dot_general | solution.py:1529
  267.0 14.2 %shard_map.358 = bf16[8,4,192,1536]{3,2,1,0:T(8,128)(2,1)} custom-call(bf16[4,512,768]{2,1,0:T(8,128)(2,1)} %get-tuple-element.158.refs_0_, bf16[512,1536]{1,0:T(8,128)(2,1)S(1)} %copy-done.2, bf16[4,512,768]{2,1,0:T(8,128)(2,1)} %get-tuple-element.163.refs_2_, bf16[512,1536]{1,0:T(8,128)(2,1)S(1)} %add_convert_fusion.2.refs_3_), custom_call_target="tpu_custom_call" | custom-call | flops 9663676416 | bytes 31457280 | tf_op jit(solution)/shard_map/pallas_call | solution.py:1036
  281.3 9.9 %multiply_reduce_fusion.1 = (bf16[1536]{0:T(1024)(128)(2,1)S(1)}, f32[512]{0:T(512)S(1)}, f32[512]{0:T(512)S(1)}, bf16[1536]{0:T(1024)(128)(2,1)S(1)}, f32[512,1536]{1,0:T(8,128)S(1)}) fusion(f32[512,1536]{1,0:T(8,128)} %copy-done.11, f32[512]{0:T(512)S(1)} %add_rsqrt_fusion, f32[512]{0:T(512)S(1)} %broadcast_multiply_fusion.5, f32[1536]{0:T(1024)S(1)} %copy-done.23, ...), kind=kOutput, calls=%fused_computation.51 | convolution fusion | flops 4838912000 | bytes 18894848 | tf_op jit(solution)/shard_map/zrn,znd->rd/dot_general | solution.py:1533
  291.2 2.6 fusion.71
  293.8 7.5 %fusion.57.dmix_ref = bf16[4,512,384]{2,1,0:T(8,128)(2,1)} fusion(bf16[512,1536]{1,0:T(8,128)(2,1)S(1)} %get-tuple-element.87.refs_1_, bf16[4,2560,1536]{2,1,0:T(8,128)(2,1)} %get-tuple-element.82), kind=kOutput, calls=%fused_computation.80 | convolution fusion | flops 2416705536 | bytes 7864320 | tf_op jit(solution)/shard_map/rd,znd->zrn/dot_general | solution.py:1541
  301.3 25.6 %shard_map.359 = (bf16[4,512,128]{2,1,0:T(8,128)(2,1)S(1)}, f32[4,8,128]{2,1,0:T(8,128)S(1)}, bf16[4,1024,512]{2,1,0:T(8,128)(2,1)}, bf16[4,1536,128]{2,1,0:T(8,128)(2,1)S(1)}) custom-call(bf16[4,512,128]{2,1,0:T(8,128)(2,1)S(1)} %get-tuple-element.141.qw_ref, bf16[4,512,128]{2,1,0:T(8,128)(2,1)S(1)} %get-tuple-element.140.qr_ref, ...), custom_call_target="tpu_custom_call" | custom-call | tf_op jit(solution)/shard_map/pallas_call | solution.py:179
  326.9 3.1 constant_dynamic-slice_fusion
  330.6 0.8 slice_reduce_fusion.1
  331.4 11.2 %fusion.40 = bf16[512,1536]{1,0:T(8,128)(2,1)} fusion(f32[512,1536]{1,0:T(8,128)} %copy-done.11, bf16[4,512,768]{2,1,0:T(8,128)(2,1)} %get-tuple-element.158.refs_0_, bf16[4,2560,1536]{2,1,0:T(8,128)(2,1)} %get-tuple-element.82), kind=kOutput, calls=%fused_computation.62 | convolution fusion | flops 4833411072 | bytes 17301504 | tf_op jit(solution)/shard_map/zrn,znd->rd/dot_general | solution.py:1523
  342.7 2.3 collective-permute-start.1
  345.6 2.4 add_convert_fusion
  348.2 9.7 %multiply_reduce_fusion.2 = (bf16[1536]{0:T(1024)(128)(2,1)S(1)}, f32[512]{0:T(512)S(1)}, f32[512]{0:T(512)S(1)}, bf16[1536]{0:T(1024)(128)(2,1)S(1)}, f32[512,1536]{1,0:T(8,128)}) fusion(f32[512,1536]{1,0:T(8,128)S(1)} %copy-done.9, f32[512]{0:T(512)S(1)} %copy-done.32, f32[512]{0:T(512)S(1)} %copy-done.29, f32[1536]{0:T(1024)S(1)} %copy-done.27, ...), kind=kOutput, calls=%fused_computation.52 | convolution fusion | flops 4038848512 | bytes 16797696 | tf_op jit(solution)/shard_map/zrn,znd->rd/dot_general | solution.py:1550
  358.7 1.4 pad.11.refs_4_
  360.0 1.8 pad_maximum_fusion.5.refs_2_
  361.8 1.2 copy-done.16
  363.0 4.2 add_convert_fusion.1.grad_ref
  367.3 11.2 %shard_map.360 = bf16[8,4,144,1536]{3,2,1,0:T(8,128)(2,1)} custom-call(bf16[4,512,384]{2,1,0:T(8,128)(2,1)S(1)} %copy-done.6, bf16[512,1536]{1,0:T(8,128)(2,1)S(1)} %copy-done.4, bf16[4,512,640]{2,1,0:T(8,128)(2,1)} %pad_maximum_fusion.5.refs_2_, bf16[512,1536]{1,0:T(8,128)(2,1)} %copy-done.21, bf16[8,4,16,1536]{3,2,1,0:T(8,128)(2,1)} %pad.11.refs_4_), custom_call_target="tpu_custom_call" | custom-call | flops 6442450944 | bytes 31457280 | tf_op jit(solution)/shard_map/pallas_call | solution.py:1036
  378.5 119.6 %shard_map.361 = (f32[2,1024,384]{2,1,0:T(8,128)}, bf16[2,1024,384]{2,1,0:T(8,128)(2,1)}, bf16[1920,1536]{1,0:T(8,128)(2,1)}, bf16[4,144,1536]{2,1,0:T(8,128)(2,1)}, bf16[4,2,2,144,1536]{4,3,2,1,0:T(8,128)(2,1)}) custom-call(bf16[512,1536]{1,0:T(8,128)(2,1)} %add_convert_fusion.1.grad_ref, bf16[2,1024,1920]{2,1,0:T(8,128)(2,1)} %get-tuple-element.90.act_ref, ...), custom_call_target="tpu_custom_call" | custom-call | tf_op jit(solution)/shard_map/pallas_call | solution.py:960
  498.2 4.0 multiply_reduce_fusion
  502.3 1.1 collective-permute-done.3
  503.5 1.0 collective-permute-start.4
  504.4 1.5 collective-permute-done.4
  506.0 1.0 collective-permute-start.5
  506.9 1.5 collective-permute-done.5
  509.1 2.4 fusion.39
  511.5 11.5 %scatter_custom_fusion = f32[2048,384]{1,0:T(8,128)} fusion(s32[2048]{0:T(1024)} %bitcast.130, f32[2048,384]{1,0:T(8,128)S(1)} %fusion.39, bf16[2048,384]{1,0:T(8,128)(2,1)} %bitcast.126, f32[]{:T(128)} %constant.72.clone.1), kind=kCustom, calls=%fused_computation.43 | custom fusion | flops 1572864 | bytes 7864832 | tf_op jit(solution)/shard_map/scatter | solution.py:1590
  523.0 4.5 pad_maximum_fusion.4.part_ref
  527.6 125.2 %shard_map.362 = (bf16[1920,1536]{1,0:T(8,128)(2,1)}, bf16[8,336,1536]{2,1,0:T(8,128)(2,1)}) custom-call(bf16[1920,1536]{1,0:T(8,128)(2,1)} %get-tuple-element.96.conv_ref, bf16[4,336,1536]{2,1,0:T(8,128)(2,1)} %pad_maximum_fusion.4.part_ref), custom_call_target="tpu_custom_call" | custom-call | tf_op jit(solution)/shard_map/pallas_call | solution.py:1256
  652.8 17.3 %shard_map.363 = (f32[1920,1536]{1,0:T(8,128)}, f32[768,1536]{1,0:T(8,128)}, f32[1536,768]{1,0:T(8,128)}, f32[384,1536]{1,0:T(8,128)}, f32[1536,128]{1,0:T(8,128...) custom-call(bf16[1920,1536]{1,0:T(8,128)(2,1)} %get-tuple-element.98.conv_ref, ...), custom_call_target="tpu_custom_call" | custom-call | tf_op jit(solution)/shard_map/pallas_call | solution.py:1327
  672.8 2.7 copy.95
  (141 shorter events, 13.6 us)
Async XLA Ops:
  7.2 5.9 copy-start
  7.2 515.8 %reduce-scatter.2.cloned.1.call-start = ((), (), s32[]{:S(2)}) async-start(), calls=%async_computation.1 | async-start | bytes 21233664 | tf_op jit(solution)/shard_map/reduce_scatter | solution.py:1428
  11.1 0.6 copy-start.25
  13.1 9.1 %copy-start.19 = (bf16[384,1536]{1,0:T(8,128)(2,1)S(1)}, bf16[384,1536]{1,0:T(8,128)(2,1)}, u32[]{:S(2)}) copy-start(bf16[384,1536]{1,0:T(8,128)(2,1)} %param.41) | copy-start | bytes 3538948
  13.1 9.1 %copy-start.37 = (f32[768]{0:T(1024)S(1)}, f32[768]{0:T(1024)}, u32[]{:S(2)}) copy-start(f32[768]{0:T(1024)} %param.45) | copy-start | bytes 9220
  195.0 2.8 copy-start.7
  195.0 3.3 copy-start.26
  195.0 3.3 copy-start.34
  197.8 1.1 copy-start.28
  198.3 0.6 copy-start.31
  198.9 9.9 %copy-start.21 = (bf16[512,1536]{1,0:T(8,128)(2,1)}, bf16[512,1536]{1,0:T(8,128)(2,1)S(1)}, u32[]{:S(2)}) copy-start(bf16[512,1536]{1,0:T(8,128)(2,1)S(1)} %add_convert_fusion.3.refs_3_) | copy-start | bytes 4718596
  208.8 2.6 copy-start.22
  211.3 4.5 collective-permute-start
  213.9 1.8 copy-start.17
  221.2 19.1 %copy-start.8 = (f32[512,1536]{1,0:T(8,128)S(1)}, f32[512,1536]{1,0:T(8,128)}, u32[]{:S(2)}) copy-start(f32[512,1536]{1,0:T(8,128)} %get-tuple-element.81) | copy-start | bytes 9437188
  240.3 5.2 copy-start.5
  245.5 11.3 %copy-start.11 = (f32[512,1536]{1,0:T(8,128)}, f32[512,1536]{1,0:T(8,128)S(1)}, u32[]{:S(2)}) copy-start(f32[512,1536]{1,0:T(8,128)S(1)} %get-tuple-element.157) | copy-start | bytes 9437188
  245.6 0.7 copy-start.23
  245.6 0.8 copy-start.35
  246.0 0.9 copy-start.33
  246.9 9.9 %copy-start.2 = (bf16[512,1536]{1,0:T(8,128)(2,1)S(1)}, bf16[512,1536]{1,0:T(8,128)(2,1)}, u32[]{:S(2)}) copy-start(bf16[512,1536]{1,0:T(8,128)(2,1)} %get-tuple-element.85.refs_1_) | copy-start | bytes 4718596
  281.3 9.9 %copy-start.12 = (f32[512,1536]{1,0:T(8,128)S(1)}, f32[512,1536]{1,0:T(8,128)}, u32[]{:S(2)}) copy-start(f32[512,1536]{1,0:T(8,128)} %copy-done.11) | copy-start | bytes 9437188
  293.8 7.5 %copy-start.3 = (bf16[512,1536]{1,0:T(8,128)(2,1)}, bf16[512,1536]{1,0:T(8,128)(2,1)S(1)}, u32[]{:S(2)}) copy-start(bf16[512,1536]{1,0:T(8,128)(2,1)S(1)} %get-tuple-element.87.refs_1_) | copy-start | bytes 4718596
  330.0 15.6 %collective-permute-start.2 = (bf16[4,512,512]{2,1,0:T(8,128)(2,1)}, bf16[4,512,512]{2,1,0:T(8,128)(2,1)}, u32[]{:S(2)}, u32[]{:S(2)}) collective-permute-start(bf16[4,512,512]{2,1,0:T(8,128)(2,1)} %constant_dynamic-slice_fusion), channel_id=1, source_target_pairs={{0,4},{1,5},{2,6},{3,7},{4,0},{5,1},{6,2},{7,3},{8,12},{9,13},{10,... | collective-permute-start | bytes 6291464 | tf_op jit(solution)/shard_map/ppermute | solution.py:1409
  331.4 13.6 %copy-start.18 = (bf16[1536,192,1]{0,1,2:T(8,128)(2,1)S(1)}, bf16[1536,192,1]{0,1,2:T(8,128)(2,1)}, u32[]{:S(2)}) copy-start(bf16[1536,192,1]{0,1,2:T(8,128)(2,1)} %copy-done.17) | copy-start | bytes 1769476
  331.4 14.2 %copy-start.20 = (bf16[4,1024,512]{2,1,0:T(8,128)(2,1)S(1)}, bf16[4,1024,512]{2,1,0:T(8,128)(2,1)}, u32[]{:S(2)}) copy-start(bf16[4,1024,512]{2,1,0:T(8,128)(2,1)} %get-tuple-element.89) | copy-start | bytes 12582916
  342.7 164.3 %collective-permute-start.1 = (bf16[512,1536]{1,0:T(8,128)(2,1)}, bf16[512,1536]{1,0:T(8,128)(2,1)}, u32[]{:S(2)}, u32[]{:S(2)}) collective-permute-start(bf16[512,1536]{1,0:T(8,128)(2,1)} %fusion.40), channel_id=1, source_target_pairs={{0,0},{1,2},{2,4},{3,6},{4,1},{5,3},{6,5},{7,7},{8,8},{9,10},{10,1... | collective-permute-start | bytes 4718600 | tf_op jit(solution)/shard_map/ppermute | solution.py:1409
  345.5 2.6 copy-start.9
  345.5 2.6 copy-start.27
  345.5 2.6 copy-start.29
  345.5 2.6 copy-start.32
  358.6 3.2 copy-start.10
  358.6 4.4 copy-start.16
  363.0 4.2 copy-start.4
  363.0 4.2 copy-start.6
  378.5 119.7 %copy-start.14 = (bf16[2048,384]{1,0:T(8,128)(2,1)S(1)}, bf16[2048,384]{1,0:T(8,128)(2,1)}, u32[]{:S(2)}) copy-start(bf16[2048,384]{1,0:T(8,128)(2,1)} %gather_fusion) | copy-start | bytes 4718596
  378.5 119.7 %copy-start.24 = (f32[384]{0:T(512)S(1)}, f32[384]{0:T(512)}, u32[]{:S(2)}) copy-start(f32[384]{0:T(512)} %param.31) | copy-start | bytes 4612
  378.5 119.7 %copy-start.30 = (f32[384]{0:T(512)S(1)}, f32[384]{0:T(512)}, u32[]{:S(2)}) copy-start(f32[384]{0:T(512)} %param.32) | copy-start | bytes 4612
  498.2 10.9 %copy-start.15 = (f32[2,1024,384]{2,1,0:T(8,128)S(1)}, f32[2,1024,384]{2,1,0:T(8,128)}, u32[]{:S(2)}) copy-start(f32[2,1024,384]{2,1,0:T(8,128)} %get-tuple-element.95) | copy-start | bytes 9437188
  502.2 1.2 collective-permute-start.3
  503.5 2.5 collective-permute-start.4
  506.0 2.5 collective-permute-start.5
  509.1 2.4 copy-start.36
  652.7 22.7 %copy-start.1 = (bf16[2048,384]{1,0:T(8,128)(2,1)S(1)}, bf16[2048,384]{1,0:T(8,128)(2,1)}, u32[]{:S(2)}) copy-start(bf16[2048,384]{1,0:T(8,128)(2,1)} %param.28) | copy-start | bytes 4718596
Sparse Core Ops, SparseCore 0:
  281.4 126.4 reduce-scatter.1
